TPU v7x, 32 devices: a whole 2x2x4 slice. The times are simulated.
32 devices in a mesh: gz: 32 (over z, y, x, core).
Axes of the slice: x: 2, y: 2, z: 4, core: 2. Of those that a mesh axis runs over, the one named last changes fastest.
Arguments:
- order_param: float32 [32, 512, 512], P('gz'), may hold values from 0.05 to 0.95
- concentration: float32 [32, 512, 512], P('gz'), may hold values from 0 to 1
- strain: float32 [6, 32, 512, 512], P(None, 'gz'), may hold values from -6 to 6
- grain_ids: int32 [32, 512, 512], P('gz'), may hold values from 0 to 15
- seed_labels: int32 [32, 512, 512], P('gz'), may hold values from 0 to 8
- grain_moduli: float32 [2, 16], replicated, may hold values from 0.5 to 2
- grain_mobility: float32 [16], replicated, may hold values from 0.25 to 1
- seed_rate: float32 [8], replicated, may hold values from 0.5 to 4
Outputs:
- order_next: float32 [32, 512, 512], P('gz')
- conc_next: float32 [32, 512, 512], P('gz')
- strain_next: float32 [6, 32, 512, 512], P(None, 'gz')
Inputs may be any that keep to these rules, and one draw needn't show every extreme that they name: `seed_labels`: 0 marks a voxel without seed; label k > 0 names entry k - 1 of seed_rate.
All inputs are finite; a program needn't handle non-finite values.
Results may differ from a plain program's by a relative error of at most 0.0003.
Values sent between devices are 32-bit elements; how exact they have to be, the bound alone decides.
A program may use at most 256 MiB of HBM per device.

v0:
```python
import math

import jax
import jax.numpy as jnp
from jax import lax
from jax.sharding import PartitionSpec as P

SUBSTEPS = 2


time_step = 0.05
grad_coef = 1.0
well_height = 1.0
drive_coef = 2.0
conc_eq = 0.5
mech_boost = 1.0
diffusivity = 1.0
release_coef = 1.0
residual_stiff = 0.1
lame_ref = 1.0
shear_ref = 1.0
coupling = (lame_ref + shear_ref) / (shear_ref * (lame_ref + 2.0 * shear_ref))


def with_halo(cells, sides, width):
    for axis, dim in sides:
        count = lax.axis_size(axis)
        head = lax.slice_in_dim(cells, 0, width, axis=dim)
        tail = lax.slice_in_dim(cells, cells.shape[dim] - width, cells.shape[dim], axis=dim)
        cells = jnp.concatenate(
            [
                lax.ppermute(tail, axis, [(i, (i + 1) % count) for i in range(count)]),
                cells,
                lax.ppermute(head, axis, [((i + 1) % count, i) for i in range(count)]),
            ],
            axis=dim,
        )
    return cells


def product(form, left, right):
    return jnp.einsum(form, left, right, precision=lax.Precision.HIGHEST)


def lookup(labels, table, first):
    count = table.shape[0]
    values = jnp.arange(count, dtype=jnp.int32) + first
    hits = labels[None] == values[:, None, None, None]
    return jnp.sum(jnp.where(hits, table[:, None, None, None], 0.0), axis=0)


def laplace_ext(extended):
    center = extended[1:-1]
    z_sum = extended[:-2] + extended[2:]
    y_sum = jnp.roll(center, 1, 1) + jnp.roll(center, -1, 1)
    x_sum = jnp.roll(center, 1, 2) + jnp.roll(center, -1, 2)
    return z_sum + y_sum + x_sum - 6.0 * center


def advance(order_ext, conc_ext, kinetic, decay):
    order_now = order_ext[1:-1]
    conc_now = conc_ext[1:-1]
    lap_order = laplace_ext(order_ext)
    lap_conc = laplace_ext(conc_ext)
    well_grad = 2.0 * order_now * (1.0 - order_now) * (1.0 - 2.0 * order_now)
    interp_grad = 6.0 * order_now * (1.0 - order_now)
    force = (
        grad_coef * lap_order
        - well_height * well_grad
        + drive_coef * interp_grad * (conc_now - conc_eq)
    )
    order_new = order_now + kinetic * force - decay * order_now
    conc_new = (
        conc_now + time_step * diffusivity * lap_conc + release_coef * (order_now - order_new)
    )
    return (order_new, conc_new)


def dft_table(length, count, weighted):
    rows = lax.broadcasted_iota(jnp.int32, (length, count), 0)
    cols = lax.broadcasted_iota(jnp.int32, (length, count), 1)
    phase = (rows * cols % max(length, count)).astype(jnp.float32) * (
        2.0 * math.pi / max(length, count)
    )
    cosine = jnp.cos(phase)
    sine = jnp.sin(phase)
    if weighted:
        weight = jnp.where(rows == 0, 1.0, 2.0)
        cosine = cosine * weight
        sine = sine * weight
    return (cosine, sine)


def signed_waves(index, count):
    return jnp.where(index < count // 2, index, index - count).astype(jnp.float32)


def green(tau, xi_x, xi_y, xi_z, limit):
    t_xx, t_yy, t_zz, t_yz, t_xz, t_xy = tau
    v_x = t_xx * xi_x + t_xy * xi_y + t_xz * xi_z
    v_y = t_xy * xi_x + t_yy * xi_y + t_yz * xi_z
    v_z = t_xz * xi_x + t_yz * xi_y + t_zz * xi_z
    inner = xi_x * v_x + xi_y * v_y + xi_z * v_z
    wave_sq = xi_x * xi_x + xi_y * xi_y + xi_z * xi_z
    live = (wave_sq > 0.5) & (xi_x < limit)
    safe_sq = jnp.where(live, wave_sq, 1.0)
    first = jnp.where(live, 1.0 / (2.0 * shear_ref * safe_sq), 0.0)
    second = jnp.where(live, coupling / (safe_sq * safe_sq), 0.0)
    xis = (xi_x, xi_y, xi_z)
    vees = (v_x, v_y, v_z)
    pairs = ((0, 0), (1, 1), (2, 2), (1, 2), (0, 2), (0, 1))
    result = []
    for left, right in pairs:
        term = (xis[right] * vees[left] + xis[left] * vees[right]) * first - xis[left] * xis[
            right
        ] * inner * second
        result.append(term)
    return result


def plane_spectra(stress_part, cos_x, sin_x, cos_y, sin_y):
    real_part = product("czyx,xk->czyk", stress_part, cos_x)
    imag_part = -product("czyx,xk->czyk", stress_part, sin_x)
    real_y = product("czyk,yq->czqk", real_part, cos_y) + product("czyk,yq->czqk", imag_part, sin_y)
    imag_y = product("czyk,yq->czqk", imag_part, cos_y) - product("czyk,yq->czqk", real_part, sin_y)
    return jnp.stack([real_y, imag_y])


def shards(
    order_param,
    concentration,
    strain,
    grain_ids,
    seed_labels,
    grain_moduli,
    grain_mobility,
    seed_rate,
):
    lame = lookup(grain_ids, grain_moduli[0], 0)
    shear = lookup(grain_ids, grain_moduli[1], 0)
    mobility = lookup(grain_ids, grain_mobility, 0)
    rate = lookup(seed_labels, seed_rate, 1)
    trace = strain[0] + strain[1] + strain[2]
    square = (
        strain[0] * strain[0]
        + strain[1] * strain[1]
        + strain[2] * strain[2]
        + 2.0 * (strain[3] * strain[3] + strain[4] * strain[4] + strain[5] * strain[5])
    )
    energy = 0.5 * lame * trace * trace + shear * square
    mech = 1.0 + mech_boost * energy / (1.0 + energy)
    kinetic = time_step * mobility * mech
    decay = time_step * rate
    order_now = order_param
    conc_now = concentration
    for step_index in range(SUBSTEPS):
        extended = with_halo(jnp.stack([order_now, conc_now]), (("gz", 1),), 1)
        order_now, conc_now = advance(extended[0], extended[1], kinetic, decay)
    scale = order_now * order_now * (3.0 - 2.0 * order_now) + residual_stiff
    lame_now = scale * lame
    shear_now = scale * shear
    parts = []
    for comp in range(6):
        if comp < 3:
            parts.append(lame_now * trace + 2.0 * shear_now * strain[comp])
        else:
            parts.append(2.0 * shear_now * strain[comp])
    stress = jnp.stack(parts)
    planes = strain.shape[1]
    width_y = strain.shape[2]
    width_x = strain.shape[3]
    half_x = width_x // 2
    devices = lax.axis_size("gz")
    depth = planes * devices
    band = width_y // devices
    cos_x, sin_x = dft_table(width_x, half_x, False)
    cos_y, sin_y = dft_table(width_y, width_y, False)
    cos_z, sin_z = dft_table(depth, depth, False)
    back_cos_x, back_sin_x = dft_table(half_x, width_x, True)
    spectral = lax.all_to_all(
        plane_spectra(stress, cos_x, sin_x, cos_y, sin_y),
        "gz",
        split_axis=3,
        concat_axis=2,
        tiled=True,
    )
    real_z = product("cznk,zw->cwnk", spectral[0], cos_z) + product(
        "cznk,zw->cwnk", spectral[1], sin_z
    )
    imag_z = product("cznk,zw->cwnk", spectral[1], cos_z) - product(
        "cznk,zw->cwnk", spectral[0], sin_z
    )
    xi_z = signed_waves(jnp.arange(depth, dtype=jnp.int32), depth)[:, None, None]
    band_rows = lax.axis_index("gz") * band + jnp.arange(band, dtype=jnp.int32)
    xi_y = signed_waves(band_rows, width_y)[None, :, None]
    xi_x = jnp.arange(half_x, dtype=jnp.int32).astype(jnp.float32)[None, None, :]
    tau = [jnp.stack([real_z[comp], imag_z[comp]]) for comp in range(6)]
    updated = jnp.stack(green(tau, xi_x, xi_y, xi_z, float(half_x)), axis=1)
    back_real = product("cwnk,wz->cznk", updated[0], cos_z) - product(
        "cwnk,wz->cznk", updated[1], sin_z
    )
    back_imag = product("cwnk,wz->cznk", updated[1], cos_z) + product(
        "cwnk,wz->cznk", updated[0], sin_z
    )
    returned = lax.all_to_all(
        jnp.stack([back_real, back_imag]), "gz", split_axis=2, concat_axis=3, tiled=True
    )
    real_y = product("czqk,qy->czyk", returned[0], cos_y) - product(
        "czqk,qy->czyk", returned[1], sin_y
    )
    imag_y = product("czqk,qy->czyk", returned[1], cos_y) + product(
        "czqk,qy->czyk", returned[0], sin_y
    )
    increment = product("czyk,kx->czyx", real_y, back_cos_x) - product(
        "czyk,kx->czyx", imag_y, back_sin_x
    )
    increment = increment * (1.0 / float(width_x * width_y * depth))
    strain_next = strain - increment
    return (order_now, conc_now, strain_next)


def solution(mesh):
    return jax.shard_map(
        shards,
        mesh=mesh,
        in_specs=(
            P("gz", None, None),
            P("gz", None, None),
            P(None, "gz", None, None),
            P("gz", None, None),
            P("gz", None, None),
            P(),
            P(),
            P(),
        ),
        out_specs=(P("gz", None, None), P("gz", None, None), P(None, "gz", None, None)),
        check_vma=False,
    )
```

profile of v0, /device:TPU:0, one launch (start us, length us, event | category | flops | bytes accessed | tf_op | source)
XLA Modules:
  0.0 604.3 jit_solution(14949335385504249390)
XLA Ops:
  0.7 1.9 pad_maximum_fusion.2
  2.6 6.4 %collective-permute-start.1 = (f32[2,1,512,512]{3,2,1,0:T(8,128)S(1)}, f32[2,1,512,512]{3,2,1,0:T(8,128)S(1)}, u32[]{:S(2)}, u32[]{:S(2)}) collective-permute-start(f32[2,1,512,512]{3,2,1,0:T(8,128)S(1)} %pad_maximum_fusion.2), channel_id=1, source_target_pairs={{1,0},{2,1},{3,2},{4,3},{5,4},{6,5},{7,6},{8,7},{9,8},{10,9},{11,1... | collective-permute-start | bytes 6291464 | tf_op jit(solution)/shard_map/ppermute | solution.py:34
  9.0 1.1 slice_bitcast_fusion.30
  10.2 0.9 select_reduce_fusion.3
  11.6 1.7 slice_bitcast_fusion.10
  13.8 5.8 select_reduce_fusion.2
  19.7 12.8 %collective-permute-done.1 = f32[2,1,512,512]{3,2,1,0:T(8,128)S(1)} collective-permute-done((f32[2,1,512,512]{3,2,1,0:T(8,128)S(1)}, f32[2,1,512,512]{3,2,1,0:T(8,128)S(1)}, u32[]{:S(2)}, u32[]{:S(2)}) %collective-permute-start.1) | collective-permute-done | bytes 2097184 | tf_op jit(solution)/shard_map/ppermute | solution.py:34
  32.5 5.6 collective-permute-done
  38.1 1.3 copy-done.19
  39.5 6.2 %fusion.61 = (f32[1,1,512,512]{3,2,1,0:T(8,128)S(1)}, f32[1,1,512,512]{3,2,1,0:T(8,128)S(1)}, f32[1,1,512,512]{3,2,1,0:T(8,128)S(1)}, f32[1,1,512,512]{3,2,0,1:T(8,128)}, f32[1,1,512,512]{3,2,1,0:T(8,128)S(1)}) fusion(f32[2,1,512,512]{3,2,1,0:T(8,128)} %copy-done.18, f32[2,1,512,512]{3,2,1,0:T(8,128)} %copy-done.19, ...), kind=kLoop, calls=%fused_computation.79 | loop fusion | flops 17301504 | bytes 30408704 | tf_op jit(solution)/shard_map/add | solution.py:74
  46.6 34.9 %collective-permute-start.2 = (f32[2,1,512,512]{3,2,1,0:T(8,128)S(1)}, f32[2,1,512,512]{3,2,1,0:T(8,128)S(1)}, u32[]{:S(2)}, u32[]{:S(2)}) collective-permute-start(f32[2,1,512,512]{3,2,1,0:T(8,128)S(1)} %pad_maximum_fusion.3), channel_id=1, source_target_pairs={{0,1},{1,2},{2,3},{3,4},{4,5},{5,6},{6,7},{7,8},{8,9},{9,10},{10,1... | collective-permute-start | bytes 6291464 | tf_op jit(solution)/shard_map/ppermute | solution.py:32
  82.3 1.8 slice_bitcast_fusion.45
  84.1 1.7 slice_bitcast_fusion.47
  85.8 3.3 collective-permute-done.2
  89.1 2.6 bitcast_dynamic-update-slice_fusion.4
  93.1 7.1 %fusion.3 = f32[6,512,256]{2,1,0:T(8,128)S(1)} fusion(f32[6,1,512,512]{3,2,0,1:T(8,128)S(1)} %fusion.95), kind=kOutput, calls=%fused_computation.11 | convolution fusion | flops 4833673216 | bytes 9437184 | tf_op jit(solution)/shard_map/czyx,xk->czyk/dot_general | solution.py:42
  100.2 7.3 %fusion.1 = f32[6,512,256]{2,1,0:T(8,128)S(1)} fusion(f32[6,1,512,512]{3,2,0,1:T(8,128)S(1)} %fusion.95), kind=kOutput, calls=%fused_computation.9 | convolution fusion | flops 4833673216 | bytes 9437184 | tf_op jit(solution)/shard_map/czyx,xk->czyk/dot_general | solution.py:42
  107.4 9.4 %fusion.92 = f32[512,6,256]{2,0,1:T(8,128)S(1)} fusion(f32[6,512,256]{2,1,0:T(8,128)S(1)} %fusion.3), kind=kOutput, calls=%fused_computation.127 | convolution fusion | flops 4835508224 | bytes 6291456 | tf_op jit(solution)/shard_map/czyk,yq->czqk/dot_general | solution.py:42
  116.8 9.1 %fusion.101 = f32[512,6,256]{2,0,1:T(8,128)S(1)} fusion(f32[6,512,256]{2,1,0:T(8,128)S(1)} %fusion.3), kind=kOutput, calls=%fused_computation.142 | convolution fusion | flops 4835508224 | bytes 6291456 | tf_op jit(solution)/shard_map/czyk,yq->czqk/dot_general | solution.py:42
  126.0 9.6 %subtract_bitcast_fusion.2 = f32[1,6,1,512,256]{4,3,1,2,0:T(8,128)S(1)} fusion(f32[512,6,256]{2,0,1:T(8,128)S(1)} %fusion.92, f32[6,512,256]{2,1,0:T(8,128)S(1)} %fusion.1), kind=kOutput, calls=%fused_computation.25 | convolution fusion | flops 4837081088 | bytes 9437184 | tf_op jit(solution)/shard_map/czyk,yq->czqk/dot_general | solution.py:42
  135.5 9.4 %add_bitcast_fusion.2 = f32[1,6,1,512,256]{4,3,1,2,0:T(8,128)S(1)} fusion(f32[512,6,256]{2,0,1:T(8,128)S(1)} %fusion.101, f32[6,512,256]{2,1,0:T(8,128)S(1)} %fusion.1), kind=kOutput, calls=%fused_computation.26 | convolution fusion | flops 4837081088 | bytes 9437184 | tf_op jit(solution)/shard_map/czyk,yq->czqk/dot_general | solution.py:42
  144.9 3.1 pad_maximum_fusion
  148.0 10.3 %copy.121 = f32[2,6,1,512,256]{4,0,2,1,3:T(2,128)} copy(f32[2,6,1,512,256]{4,3,1,2,0:T(8,128)} %pad_maximum_fusion) | data formatting | bytes 12582912 | tf_op jit(solution)/shard_map/stack | solution.py:126
  158.3 46.0 %all-to-all-start = ((f32[2,6,1,512,256]{4,0,2,1,3:T(2,128)}), f32[2,6,1,512,256]{4,0,2,1,3:T(2,128)}, u32[]{:S(2)}, u32[]{:S(2)}) async-start(f32[2,6,1,512,256]{4,0,2,1,3:T(2,128)} %copy.121), calls=%async_computation | async-start | bytes 12582912 | tf_op jit(solution)/shard_map/all_to_all | solution.py:180
  205.0 139.1 %all-to-all-done = f32[2,6,1,512,256]{4,0,2,1,3:T(2,128)} async-done(((f32[2,6,1,512,256]{4,0,2,1,3:T(2,128)}), f32[2,6,1,512,256]{4,0,2,1,3:T(2,128)}, u32[]{:S(2)}, u32[]{:S(2)}) %all-to-all-start) | async-done | bytes 6291488 | tf_op jit(solution)/shard_map/all_to_all | solution.py:180
  344.1 12.7 %fusion.275 = (f32[1,6,1,512,256]{4,0,2,1,3:T(1,128)}, f32[1,6,1,512,256]{4,0,2,1,3:T(1,128)}) fusion(f32[2,6,1,512,256]{4,0,2,1,3:T(2,128)} %all-to-all-done), kind=kLoop, calls=%fused_computation.363 | loop fusion | bytes 12582912 | tf_op jit(solution)/shard_map/slice | solution.py:187
  356.8 2.2 copy.136
  359.0 4.6 fusion.15
  363.7 5.0 fusion.17
  369.0 4.7 subtract_bitcast_fusion.1
  373.9 4.8 add_bitcast_fusion.1
  378.9 1.3 subtract_dynamic-update-slice_fusion.5
  383.1 3.0 fusion.11
  386.0 3.0 fusion.12
  389.0 3.2 add_bitcast_fusion
  392.2 3.0 subtract_bitcast_fusion
  395.2 1.1 pad_maximum_fusion.1
  396.3 6.4 %copy.128 = f32[2,6,32,16,256]{4,3,1,0,2:T(8,128)} copy(f32[2,6,32,16,256]{4,2,3,1,0:T(8,128)S(1)} %pad_maximum_fusion.1) | data formatting | bytes 12582912 | tf_op jit(solution)/shard_map/stack | solution.py:206
  402.7 3.7 all-to-all-start.1
  410.3 5.9 fusion.55
  416.2 130.2 %all-to-all-done.1 = f32[2,6,32,16,256]{4,3,1,0,2:T(8,128)} async-done(((f32[2,6,32,16,256]{4,3,1,0,2:T(8,128)}), f32[2,6,32,16,256]{4,3,1,0,2:T(8,128)}, u32[]{:S(2)}, u32[]{:S(2)}) %all-to-all-start.1) | async-done | bytes 6291488 | tf_op jit(solution)/shard_map/all_to_all | solution.py:205
  546.4 3.6 fusion.274
  550.4 9.0 %fusion.88 = f32[512,6,256]{2,0,1:T(8,128)S(1)} fusion(f32[6,512,256]{2,1,0:T(8,128)S(1)} %bitcast.340), kind=kOutput, calls=%fused_computation.123 | convolution fusion | flops 4835508224 | bytes 6291456 | tf_op jit(solution)/shard_map/czqk,qy->czyk/dot_general | solution.py:42
  559.5 9.2 %fusion.98 = f32[512,6,256]{2,0,1:T(8,128)S(1)} fusion(f32[6,512,256]{2,1,0:T(8,128)S(1)} %bitcast.341), kind=kOutput, calls=%fused_computation.139 | convolution fusion | flops 4835508224 | bytes 6291456 | tf_op jit(solution)/shard_map/czqk,qy->czyk/dot_general | solution.py:42
  569.0 9.2 %fusion.96 = f32[512,6,256]{2,0,1:T(8,128)S(1)} fusion(f32[6,512,256]{2,1,0:T(8,128)S(1)} %bitcast.342), kind=kOutput, calls=%fused_computation.137 | convolution fusion | flops 4835508224 | bytes 6291456 | tf_op jit(solution)/shard_map/czqk,qy->czyk/dot_general | solution.py:42
  578.2 9.3 %fusion.90 = f32[512,6,256]{2,0,1:T(8,128)S(1)} fusion(f32[6,512,256]{2,1,0:T(8,128)S(1)} %bitcast.343), kind=kOutput, calls=%fused_computation.125 | convolution fusion | flops 4835508224 | bytes 6291456 | tf_op jit(solution)/shard_map/czqk,qy->czyk/dot_general | solution.py:42
  587.5 7.2 %fusion.5 = f32[6,512,512]{2,1,0:T(8,128)S(1)} fusion(f32[512,6,256]{2,0,1:T(8,128)S(1)} %fusion.96, f32[512,6,256]{2,0,1:T(8,128)S(1)} %fusion.88, f32[256]{0:T(256)S(1)} %compare_select_fusion.2), kind=kOutput, calls=%fused_computation.15 | convolution fusion | flops 4834590720 | bytes 12583936 | tf_op jit(solution)/shard_map/czyk,kx->czyx/dot_general | solution.py:42
  594.7 9.1 %fusion = f32[6,1,512,512]{3,2,1,0:T(8,128)} fusion(f32[6,512,512]{2,1,0:T(8,128)S(1)} %fusion.5, f32[512,6,256]{2,0,1:T(8,128)S(1)} %fusion.98, f32[512,6,256]{2,0,1:T(8,128)S(1)} %fusion.90, f32[256]{0:T(256)S(1)} %compare_select_fusion.2, f32[6,1,512,512]{3,2,1,0:T(8,128)S(1)} %bitcast.333), kind=kOutput, calls=%fused_computation.8 | convolution fusion | flops 4839309312 | bytes 25166848 | tf_op jit(solution)/shard_map/czyk,kx->czyx/dot_general | solution.py:42
  (101 shorter events, 12.8 us)
Async XLA Ops:
  0.6 8.4 %copy-start = (f32[1,512,512]{2,1,0:T(8,128)S(1)}, f32[1,512,512]{2,1,0:T(8,128)}, u32[]{:S(2)}) copy-start(f32[1,512,512]{2,1,0:T(8,128)} %param.9) | copy-start | bytes 3145732
  0.6 8.3 %copy-start.1 = (f32[1,512,512]{2,1,0:T(8,128)S(1)}, f32[1,512,512]{2,1,0:T(8,128)}, u32[]{:S(2)}) copy-start(f32[1,512,512]{2,1,0:T(8,128)} %param.8) | copy-start | bytes 3145732
  0.7 9.5 %copy-start.21 = (s32[1,512,512]{2,1,0:T(8,128)S(1)}, s32[1,512,512]{2,1,0:T(8,128)}, u32[]{:S(2)}) copy-start(s32[1,512,512]{2,1,0:T(8,128)} %param.12) | copy-start | bytes 3145732
  0.7 9.5 %copy-start.24 = (f32[8]{0:T(128)S(1)}, f32[8]{0:T(128)}, u32[]{:S(2)}) copy-start(f32[8]{0:T(128)} %param.15) | copy-start | bytes 100
  2.5 8.5 %copy-start.22 = (f32[2,16]{1,0:T(2,128)S(1)}, f32[2,16]{1,0:T(2,128)}, u32[]{:S(2)}) copy-start(f32[2,16]{1,0:T(2,128)} %param.13) | copy-start | bytes 388
  2.6 30.0 %collective-permute-start.1 = (f32[2,1,512,512]{3,2,1,0:T(8,128)S(1)}, f32[2,1,512,512]{3,2,1,0:T(8,128)S(1)}, u32[]{:S(2)}, u32[]{:S(2)}) collective-permute-start(f32[2,1,512,512]{3,2,1,0:T(8,128)S(1)} %pad_maximum_fusion.2), channel_id=1, source_target_pairs={{1,0},{2,1},{3,2},{4,3},{5,4},{6,5},{7,6},{8,7},{9,8},{10,9},{11,1... | collective-permute-start | bytes 6291464 | tf_op jit(solution)/shard_map/ppermute | solution.py:34
  9.0 29.2 %collective-permute-start = (f32[2,1,512,512]{3,2,1,0:T(8,128)S(1)}, f32[2,1,512,512]{3,2,1,0:T(8,128)S(1)}, u32[]{:S(2)}, u32[]{:S(2)}) collective-permute-start(f32[2,1,512,512]{3,2,1,0:T(8,128)S(1)} %pad_maximum_fusion.2), channel_id=1, source_target_pairs={{0,1},{1,2},{2,3},{3,4},{4,5},{5,6},{6,7},{7,8},{8,9},{9,10},{10,1... | collective-permute-start | bytes 6291464 | tf_op jit(solution)/shard_map/ppermute | solution.py:32
  11.1 78.0 %copy-start.6 = (f32[512,512]{1,0:T(8,128)}, f32[512,512]{1,0:T(8,128)S(1)}, u32[]{:S(2)}) copy-start(f32[512,512]{1,0:T(8,128)S(1)} %select_reduce_fusion.3) | copy-start | bytes 3145732
  11.1 28.4 %slice-start = ((s8[6291456]{0:T(1024)(128)(4,1)}), s8[4194304]{0:T(1024)(128)(4,1)S(1)}, s32[]{:S(2)}) async-start(s8[6291456]{0:T(1024)(128)(4,1)} %bitcast.328), calls=%async_computation.2 | async-start | bytes 8388608
  11.6 2.2 copy-start.20
  11.6 2.2 copy-start.23
  11.6 27.9 %slice-start.1 = ((s8[6291456]{0:T(1024)(128)(4,1)}), s8[2097152]{0:T(1024)(128)(4,1)S(1)}, s32[]{:S(2)}) async-start(s8[6291456]{0:T(1024)(128)(4,1)} %bitcast.328), calls=%async_computation.3 | async-start | bytes 4194304
  19.7 26.0 %copy-start.9 = (f32[512,512]{1,0:T(8,128)}, f32[512,512]{1,0:T(8,128)S(1)}, u32[]{:S(2)}) copy-start(f32[512,512]{1,0:T(8,128)S(1)} %get-tuple-element.21) | copy-start | bytes 3145732
  19.7 69.4 %copy-start.2 = (f32[512,512]{1,0:T(8,128)}, f32[512,512]{1,0:T(8,128)S(1)}, u32[]{:S(2)}) copy-start(f32[512,512]{1,0:T(8,128)S(1)} %get-tuple-element.22) | copy-start | bytes 3145732
  19.7 69.4 %copy-start.4 = (f32[512,512]{1,0:T(8,128)}, f32[512,512]{1,0:T(8,128)S(1)}, u32[]{:S(2)}) copy-start(f32[512,512]{1,0:T(8,128)S(1)} %get-tuple-element.23) | copy-start | bytes 3145732
  32.5 5.6 copy-start.18
  38.1 1.3 copy-start.19
  45.7 43.5 %copy-start.11 = (f32[1,1,512,512]{3,2,1,0:T(8,128)}, f32[1,1,512,512]{3,2,1,0:T(8,128)S(1)}, u32[]{:S(2)}) copy-start(f32[1,1,512,512]{3,2,1,0:T(8,128)S(1)} %get-tuple-element.37) | copy-start | bytes 3145732
  45.8 40.0 %collective-permute-start.3 = (f32[2,1,512,512]{3,2,1,0:T(8,128)S(1)}, f32[2,1,512,512]{3,2,1,0:T(8,128)S(1)}, u32[]{:S(2)}, u32[]{:S(2)}) collective-permute-start(f32[2,1,512,512]{3,2,1,0:T(8,128)S(1)} %pad_maximum_fusion.3), channel_id=1, source_target_pairs={{1,0},{2,1},{3,2},{4,3},{5,4},{6,5},{7,6},{8,7},{9,8},{10,9},{11,1... | collective-permute-start | bytes 6291464 | tf_op jit(solution)/shard_map/ppermute | solution.py:34
  46.6 42.5 %collective-permute-start.2 = (f32[2,1,512,512]{3,2,1,0:T(8,128)S(1)}, f32[2,1,512,512]{3,2,1,0:T(8,128)S(1)}, u32[]{:S(2)}, u32[]{:S(2)}) collective-permute-start(f32[2,1,512,512]{3,2,1,0:T(8,128)S(1)} %pad_maximum_fusion.3), channel_id=1, source_target_pairs={{0,1},{1,2},{2,3},{3,4},{4,5},{5,6},{6,7},{7,8},{8,9},{9,10},{10,1... | collective-permute-start | bytes 6291464 | tf_op jit(solution)/shard_map/ppermute | solution.py:32
  85.8 5.9 copy-start.13
  89.1 2.6 copy-start.15
  158.3 185.8 %all-to-all-start = ((f32[2,6,1,512,256]{4,0,2,1,3:T(2,128)}), f32[2,6,1,512,256]{4,0,2,1,3:T(2,128)}, u32[]{:S(2)}, u32[]{:S(2)}) async-start(f32[2,6,1,512,256]{4,0,2,1,3:T(2,128)} %copy.121), calls=%async_computation | async-start | bytes 12582912 | tf_op jit(solution)/shard_map/all_to_all | solution.py:180
  363.6 5.0 copy-start.8
  402.7 4.6 copy-start.17
  402.7 143.7 %all-to-all-start.1 = ((f32[2,6,32,16,256]{4,3,1,0,2:T(8,128)}), f32[2,6,32,16,256]{4,3,1,0,2:T(8,128)}, u32[]{:S(2)}, u32[]{:S(2)}) async-start(f32[2,6,32,16,256]{4,3,1,0,2:T(8,128)} %copy.128), calls=%async_computation.1 | async-start | bytes 12582912 | tf_op jit(solution)/shard_map/all_to_all | solution.py:205
  406.5 1.6 copy-start.16
  406.6 1.7 copy-start.12
  406.7 2.4 copy-start.14
  406.9 2.5 copy-start.3
  406.9 2.8 copy-start.5
  406.9 3.1 copy-start.7
  406.9 3.4 copy-start.10
  578.2 16.5 %slice-start.2 = ((s8[6291456]{0:T(1024)(128)(4,1)}), s8[4194304]{0:T(1024)(128)(4,1)S(1)}, s32[]{:S(2)}) async-start(s8[6291456]{0:T(1024)(128)(4,1)} %bitcast.332), calls=%async_computation.4 | async-start | bytes 8388608
  587.5 7.2 %slice-start.3 = ((s8[6291456]{0:T(1024)(128)(4,1)}), s8[2097152]{0:T(1024)(128)(4,1)S(1)}, s32[]{:S(2)}) async-start(s8[6291456]{0:T(1024)(128)(4,1)} %bitcast.332), calls=%async_computation.5 | async-start | bytes 4194304
where the time goes:
time: 611 us; the launch traced here: 604 us
  waiting for transfers between devices  291 us (48%)
  matrix products  136 us (22%)
  starting transfers between devices  91.8 us (15%)
  local copies, waits for them, and re-layouts  50 us (8%)
  other arithmetic  33.7 us (6%)
    all_to_all x1, waiting for transfers between devices, shards(): lax.all_to_all(plane_spectra(stress, cos_x, sin_x, cos_y, sin_y), 'gz', s...  139 us
    dot_general x20, matrix products, product(): return jnp.einsum(form, left, right, precision=lax.Precision.HIGHEST)  136 us
    all_to_all x1, waiting for transfers between devices, shards(): lax.all_to_all(jnp.stack([back_real, back_imag]), 'gz', split_axis=2, con...  130 us
    all_to_all x1, starting transfers between devices, shards(): lax.all_to_all(plane_spectra(stress, cos_x, sin_x, cos_y, sin_y), 'gz', s...  46 us
    ppermute x2, starting transfers between devices, with_halo(): lax.ppermute(tail, axis, [(i, (i + 1) % count) for i in range(count)])  34.9 us
    ppermute x2, waiting for transfers between devices, with_halo(): lax.ppermute(head, axis, [((i + 1) % count, i) for i in range(count)])  12.8 us
    slice x1, local copies, waits for them, and re-layouts, shards(): spectral[0]  12.7 us
  transfers between devices with their start and end apart: 6, of which 5 were waited for; matrix products, arithmetic and copies ran while one was open for 4% of the time, Pallas kernels for 0%

commit v1 on v0

v1 whole, which is shorter than its diff:
```python
import functools
import math

import jax
import jax.numpy as jnp
import numpy as np
from jax import lax
from jax.experimental import pallas as pl
from jax.experimental.pallas import tpu as pltpu
from jax.sharding import PartitionSpec as P

SUBSTEPS = 2
time_step = 0.05
conc_eq = 0.5
residual_stiff = 0.1
lame_ref = 1.0
shear_ref = 1.0
coupling = (lame_ref + shear_ref) / (shear_ref * (lame_ref + 2.0 * shear_ref))
F32 = jnp.float32
BF16 = jnp.bfloat16
LIMIT = 50 * 1024 * 1024


def lookup(labels, table, first):
    out = jnp.zeros(labels.shape, F32)
    for k in range(table.shape[0]):
        out = jnp.where(labels == k + first, table[k], out)
    return out


def neighbours(plane):
    count = lax.axis_size("gz")
    below = lax.ppermute(plane, "gz", [(i, (i + 1) % count) for i in range(count)])
    above = lax.ppermute(plane, "gz", [((i + 1) % count, i) for i in range(count)])
    return below + above


def laplace(plane, z_sum):
    y_sum = jnp.roll(plane, 1, 0) + jnp.roll(plane, -1, 0)
    x_sum = jnp.roll(plane, 1, 1) + jnp.roll(plane, -1, 1)
    return z_sum + y_sum + x_sum - 6.0 * plane


def order_step(p, c, lap, kinetic, decay):
    well = 2.0 * p * (1.0 - p) * (1.0 - 2.0 * p)
    interp = 6.0 * p * (1.0 - p)
    force = lap - well + 2.0 * interp * (c - conc_eq)
    return p + kinetic * force - decay * p


def pair(table):
    table = jnp.asarray(np.asarray(table, np.float32))
    hi = table.astype(BF16)
    return hi, (table - hi.astype(F32)).astype(BF16)


def tables(nx, ny, depth):
    hx, hy = nx // 2, ny // 2
    x = np.arange(hx)[:, None]
    y = np.arange(hy)[None, :]
    fx, ix, fy, iy = [], [], [], []
    for par in range(2):
        kx = 2 * np.arange(hx // 2)[None, :] + par
        ph = 2.0 * np.pi * ((x * kx) % nx) / nx
        fx.append(np.concatenate([np.cos(ph), -np.sin(ph)], 1))
        weight = np.where(kx == 0, 1.0, 2.0) / float(nx * ny * depth)
        ix.append(np.concatenate([np.cos(ph) * weight, -np.sin(ph) * weight], 1).T)
        ky = 2 * np.arange(hy)[:, None] + par
        ph = 2.0 * np.pi * ((ky * y) % ny) / ny
        fy.append(np.concatenate([np.cos(ph), np.sin(ph)], 0))
        iy.append(np.concatenate([np.cos(ph).T, np.sin(ph).T], 0))
    return fx, np.stack(fy), ix, np.stack(iy)


def split(x):
    hi = x.astype(BF16)
    return hi, (x - hi.astype(F32)).astype(BF16)


def dot3(a, b):
    def dot(u, v):
        return jnp.dot(u, v, preferred_element_type=F32)

    return dot(a[0], b[0]) + (dot(a[0], b[1]) + dot(a[1], b[0]))


def waves(par, ny, lanes):
    mx = (2 * lax.broadcasted_iota(jnp.int32, (1, lanes), 1) + par[0]).astype(F32)
    row = 2 * lax.broadcasted_iota(jnp.int32, (ny // 2, 1), 0) + par[1]
    my = jnp.where(row < ny // 2, row, row - ny).astype(F32)
    return mx, my


def forward_kernel(h, e_ref, lt_ref, m2_ref, xh_ref, xl_ref, yh_ref, yl_ref, o0_ref, o1_ref):
    t = pl.program_id(0)
    ny, nx = lt_ref.shape
    hy, hx, lanes = ny // 2, nx // 2, nx // 4
    diag = jnp.where((t == 0) | (t == 2) | (t == 5), 1.0, 0.0).astype(F32)
    s = m2_ref[...] * e_ref[0] + diag * lt_ref[...]
    left, right = s[:, :hx], s[:, hx:]
    folded = left + right if h == 0 else left - right
    xs = dot3(split(folded), (xh_ref[...], xl_ref[...]))
    for g, o_ref in enumerate((o0_ref, o1_ref)):
        nd, _, band, _ = o_ref.shape
        ys = xs[:hy] + xs[hy:] if g == 0 else xs[:hy] - xs[hy:]
        d = dot3((yh_ref[g], yl_ref[g]), split(ys))
        re = d[:hy, :lanes] + d[hy:, lanes:]
        im = d[:hy, lanes:] - d[hy:, :lanes]
        mx, my = waves((h, g), ny, lanes)

        def put(slot, a, b, add=False):
            a, b = a.reshape(nd, band, lanes), b.reshape(nd, band, lanes)
            if add:
                a, b = a + o_ref[:, slot], b + o_ref[:, slot + 1]
            o_ref[:, slot] = a
            o_ref[:, slot + 1] = b

        @pl.when(t == 0)
        def _():
            put(0, mx * re, mx * im)

        @pl.when(t == 1)
        def _():
            put(0, my * re, my * im, True)
            put(2, mx * re, mx * im)

        @pl.when(t == 2)
        def _():
            put(2, my * re, my * im, True)

        for k in range(3):
            @pl.when(t == 3 + k)
            def _():
                put(4 + 2 * k, re, im)


def whole(shape):
    return pl.BlockSpec(shape, lambda t: (0,) * len(shape))


def forward(h, strain, lt, m2, fx, fy, devices):
    ny, nx = lt.shape
    shape = (devices, 10, ny // 2 // devices, nx // 4)

    def comp(t):
        c = jnp.where(t == 1, 5, jnp.where(t == 2, 1, jnp.where(t >= 3, 7 - t, 0)))
        return (c, 0, 0)

    return pl.pallas_call(
        functools.partial(forward_kernel, h),
        grid=(6,),
        in_specs=[pl.BlockSpec((1, ny, nx), comp), whole((ny, nx)), whole((ny, nx))]
        + [whole(v.shape) for v in fx + fy],
        out_specs=[whole(shape)] * 2,
        out_shape=[jax.ShapeDtypeStruct(shape, F32)] * 2,
        compiler_params=pltpu.CompilerParams(vmem_limit_bytes=LIMIT),
        cost_estimate=pl.CostEstimate(
            flops=6 * 3 * 2 * (ny * nx * nx // 4 + ny * ny * nx // 2),
            bytes_accessed=14 * 1024 * 1024,
            transcendentals=0,
        ),
    )(strain, lt, m2, *fx, *fy)


def fft(re, im, sign):
    n = len(re)
    if n == 1:
        return re, im
    half = n // 2
    sr = [re[k] + re[k + half] for k in range(half)]
    si = [im[k] + im[k + half] for k in range(half)]
    dr, di = [], []
    for k in range(half):
        a, b = re[k] - re[k + half], im[k] - im[k + half]
        if k == 0:
            dr.append(a)
            di.append(b)
        elif 4 * k == n:
            dr.append(-sign * b)
            di.append(sign * a)
        else:
            c = math.cos(2.0 * math.pi * k / n)
            s = sign * math.sin(2.0 * math.pi * k / n)
            dr.append(a * c - b * s)
            di.append(a * s + b * c)
    er, ei = fft(sr, si, sign)
    orr, oi = fft(dr, di, sign)
    outr, outi = [None] * n, [None] * n
    outr[0::2], outr[1::2], outi[0::2], outi[1::2] = er, orr, ei, oi
    return outr, outi


def green_kernel(h, x_ref, my_ref, o_ref, v_ref):
    depth, _, band, lanes = x_ref.shape

    def transform(src, dst, sign):
        def body(c, carry):
            re = [src[k, 2 * c] for k in range(depth)]
            im = [src[k, 2 * c + 1] for k in range(depth)]
            re, im = fft(re, im, sign)
            for k in range(depth):
                dst[k, 2 * c] = re[k]
                dst[k, 2 * c + 1] = im[k]
            return carry

        lax.fori_loop(0, 5, body, 0)

    transform(x_ref, v_ref, -1.0)
    mx = (2 * lax.broadcasted_iota(jnp.int32, (band, lanes), 1) + h).astype(F32)
    my = my_ref[...]
    flat = mx * mx + my * my

    def body(k, carry):
        mz = jnp.where(k < depth // 2, k, k - depth).astype(F32)
        k2 = flat + mz * mz
        live = k2 > 0.5
        inv = jnp.where(live, 1.0 / jnp.where(live, k2, 1.0), 0.0)
        for part in range(2):
            wx, wy, txz, tyz, tzz = [v_ref[k, 2 * c + part] for c in range(5)]
            vx = wx + mz * txz
            vy = wy + mz * tyz
            vz = mx * txz + my * tyz + mz * tzz
            inner = (mx * vx + my * vy + mz * vz) * (coupling * inv)
            ux = (vx - mx * inner) * inv
            uy = (vy - my * inner) * inv
            uz = (vz - mz * inner) * inv
            v_ref[k, part] = ux
            v_ref[k, 2 + part] = uy
            v_ref[k, 4 + part] = 0.5 * (mx * uz + mz * ux)
            v_ref[k, 6 + part] = 0.5 * (my * uz + mz * uy)
            v_ref[k, 8 + part] = mz * uz
        return carry

    lax.fori_loop(0, depth, body, 0)
    transform(v_ref, o_ref, 1.0)


def green(h, g, chunk, ny):
    depth, _, band, lanes = chunk.shape
    row = 2 * (lax.axis_index("gz") * band + jnp.arange(band, dtype=jnp.int32)) + g
    my = jnp.where(row < ny // 2, row, row - ny).astype(F32)
    my = jnp.broadcast_to(my[:, None], (band, lanes))
    return pl.pallas_call(
        functools.partial(green_kernel, h),
        in_specs=[pl.BlockSpec(memory_space=pltpu.VMEM)] * 2,
        out_specs=pl.BlockSpec(memory_space=pltpu.VMEM),
        out_shape=jax.ShapeDtypeStruct(chunk.shape, F32),
        scratch_shapes=[pltpu.VMEM(chunk.shape, F32)],
        compiler_params=pltpu.CompilerParams(vmem_limit_bytes=LIMIT),
        cost_estimate=pl.CostEstimate(
            flops=chunk.size * 64, bytes_accessed=chunk.size * 8, transcendentals=0
        ),
    )(chunk, my)


def inverse_kernel(h, r0_ref, r1_ref, xh_ref, xl_ref, yh_ref, yl_ref, *rest):
    g_ref = rest[-1]
    t = pl.program_id(0)
    lanes = r0_ref.shape[3]
    hy = r0_ref.shape[0] * r0_ref.shape[2]
    sums = []
    for g, r_ref in enumerate((r0_ref, r1_ref)):
        mx, my = waves((h, g), 2 * hy, lanes)

        def get(slot):
            return [r_ref[:, slot + part].reshape(hy, lanes) for part in range(2)]

        def put(a, b):
            g_ref[:, :lanes] = a
            g_ref[:, lanes:] = b

        @pl.when(t == 0)
        def _():
            a, b = get(0)
            put(mx * a, mx * b)

        @pl.when(t == 1)
        def _():
            a, b = get(2)
            put(my * a, my * b)

        @pl.when(t == 5)
        def _():
            a, b = get(0)
            c, d = get(2)
            put(0.5 * (my * a + mx * c), 0.5 * (my * b + mx * d))

        @pl.when((t >= 2) & (t <= 4))
        def _():
            put(*get(2 * (6 - t)))

        d = dot3((yh_ref[g], yl_ref[g]), split(g_ref[...]))
        re = d[:hy, :lanes] - d[hy:, lanes:]
        im = d[:hy, lanes:] + d[hy:, :lanes]
        sums.append(jnp.concatenate([re, im], axis=1))
    full = jnp.concatenate([sums[0] + sums[1], sums[0] - sums[1]], axis=0)
    z = dot3(split(full), (xh_ref[...], xl_ref[...]))
    if h == 0:
        rest[0][0] = z
    else:
        z0_ref, e_ref, o_ref = rest[:3]
        hx = z.shape[1]
        z0 = z0_ref[0]
        o_ref[0, :, :hx] = e_ref[0, :, :hx] - (z0 + z)
        o_ref[0, :, hx:] = e_ref[0, :, hx:] - (z0 - z)


def inverse(h, r0, r1, ix, iy, ny, nx, extra=()):
    def plane(width):
        return pl.BlockSpec((1, ny, width), lambda t: (t, 0, 0))

    width = nx // 2 if h == 0 else nx
    return pl.pallas_call(
        functools.partial(inverse_kernel, h),
        grid=(6,),
        in_specs=[whole(v.shape) for v in (r0, r1) + ix + iy]
        + [plane(v.shape[2]) for v in extra],
        out_specs=plane(width),
        out_shape=jax.ShapeDtypeStruct((6, ny, width), F32),
        scratch_shapes=[pltpu.VMEM((ny // 2, nx // 2), F32)],
        compiler_params=pltpu.CompilerParams(vmem_limit_bytes=LIMIT),
        cost_estimate=pl.CostEstimate(
            flops=6 * 3 * 2 * (ny * nx * nx // 4 + ny * ny * nx // 2),
            bytes_accessed=14 * 1024 * 1024,
            transcendentals=0,
        ),
    )(r0, r1, *ix, *iy, *extra)


def shards(
    order_param,
    concentration,
    strain,
    grain_ids,
    seed_labels,
    grain_moduli,
    grain_mobility,
    seed_rate,
):
    devices = lax.axis_size("gz")
    ny, nx = strain.shape[2], strain.shape[3]
    fx, fy, ix, iy = tables(nx, ny, devices)
    fx, ix = [pair(v) for v in fx], [pair(v) for v in ix]
    fy, iy = pair(fy), pair(iy)
    strain = strain.reshape(6, ny, nx)
    p, c = order_param[0], concentration[0]
    p_sum = neighbours(p)
    c_sum = neighbours(c)
    ids, seeds = grain_ids[0], seed_labels[0]
    lame = lookup(ids, grain_moduli[0], 0)
    shear = lookup(ids, grain_moduli[1], 0)
    mobility = lookup(ids, grain_mobility, 0)
    rate = lookup(seeds, seed_rate, 1)
    trace = strain[0] + strain[1] + strain[2]
    square = (
        strain[0] * strain[0]
        + strain[1] * strain[1]
        + strain[2] * strain[2]
        + 2.0 * (strain[3] * strain[3] + strain[4] * strain[4] + strain[5] * strain[5])
    )
    energy = 0.5 * lame * trace * trace + shear * square
    kinetic = time_step * mobility * (1.0 + energy / (1.0 + energy))
    decay = time_step * rate
    p1 = order_step(p, c, laplace(p, p_sum), kinetic, decay)
    p1_sum = neighbours(p1)
    c1 = c + time_step * laplace(c, c_sum) + (p - p1)
    p2 = order_step(p1, c1, laplace(p1, p1_sum), kinetic, decay)
    scale = p2 * p2 * (3.0 - 2.0 * p2) + residual_stiff
    lt = scale * lame * trace
    m2 = 2.0 * (scale * shear)

    sent = [list(forward(h, strain, lt, m2, fx[h], fy, devices)) for h in range(2)]
    c1_late, sent[0][0] = lax.optimization_barrier((c1, sent[0][0]))
    c1_sum = neighbours(c1_late)
    c2 = c1_late + time_step * laplace(c1_late, c1_sum) + (p1 - p2)

    def swap(chunk):
        return lax.all_to_all(chunk, "gz", split_axis=0, concat_axis=0, tiled=True)

    back = [[swap(green(h, g, swap(sent[h][g]), ny)) for g in range(2)] for h in range(2)]
    z0 = inverse(0, back[0][0], back[0][1], ix[0], iy, ny, nx)
    out = inverse(1, back[1][0], back[1][1], ix[1], iy, ny, nx, (z0, strain))
    return (p2[None], c2[None], out[:, None])


def solution(mesh):
    return jax.shard_map(
        shards,
        mesh=mesh,
        in_specs=(
            P("gz", None, None),
            P("gz", None, None),
            P(None, "gz", None, None),
            P("gz", None, None),
            P("gz", None, None),
            P(),
            P(),
            P(),
        ),
        out_specs=(P("gz", None, None), P("gz", None, None), P(None, "gz", None, None)),
        check_vma=False,
    )
```

time: 611 us -> 482 us (0.79)
  matrix products: 136 us -> 0 us
  waiting for transfers between devices: 291 us -> 176 us
  blocking collectives: 0 us -> 88.9 us
  Pallas kernels: 0 us -> 54.1 us
  other arithmetic: 33.7 us -> 79.8 us
  starting transfers between devices: 91.8 us -> 53.6 us
  local copies, waits for them, and re-layouts: 50 us -> 23.4 us
    all_to_all x2 -> x6, waiting for transfers between devices: 269 us -> 133 us  [swap(): return lax.all_to_all(chunk, 'gz', split_axis=0, concat_axis=0, tiled=True)]
    dot_general x20 -> x0, matrix products: 136 us -> none  [product(): return jnp.einsum(form, left, right, precision=lax.Precision.HIGHEST)]
    all_to_all x0 -> x2, blocking collectives: none -> 88.9 us  [swap(): return lax.all_to_all(chunk, 'gz', split_axis=0, concat_axis=0, tiled=True)]
    pallas_call x0 -> x8, Pallas kernels: none -> 54.1 us  [the longest x2 24.5 us: forward(): pl.pallas_call(functools.partial(forward_kernel, h), grid=(6,), in_specs=...]
    sub x0 -> x1, other arithmetic: none -> 42.9 us  [order_step(): return p + kinetic * force - decay * p]
    mul x6 -> x2, other arithmetic: 0.24 us -> 34.6 us  [the longest x1 22.4 us: shards(): m2 = 2.0 * (scale * shear)]
    all_to_all x2 -> x6, starting transfers between devices: 49.7 us -> 20.3 us  [swap(): return lax.all_to_all(chunk, 'gz', split_axis=0, concat_axis=0, tiled=True)]
    ppermute x4 -> x8, waiting for transfers between devices: 21.7 us -> 43.1 us  [the longest x4 33.1 us: neighbours(): lax.ppermute(plane, 'gz', [(i, (i + 1) % count) for i in range(count)])]
  transfers between devices with their start and end apart: 6 -> 14, of which waited for: 5 -> 9; matrix products, arithmetic and copies ran while one was open for 4% -> 11% of each run, Pallas kernels for 0% -> 6%
where the time goes in v1:
time: 482 us; the launch traced here: 477 us
  waiting for transfers between devices  176 us (37%)
  blocking collectives  88.9 us (18%)
  other arithmetic  79.8 us (17%)
  Pallas kernels  54.1 us (11%)
  starting transfers between devices  53.6 us (11%)
  local copies, waits for them, and re-layouts  23.4 us (5%)
    all_to_all x6, waiting for transfers between devices, swap(): return lax.all_to_all(chunk, 'gz', split_axis=0, concat_axis=0, tiled=True)  133 us
    all_to_all x2, blocking collectives, swap(): return lax.all_to_all(chunk, 'gz', split_axis=0, concat_axis=0, tiled=True)  88.9 us
    sub x1, other arithmetic, order_step(): return p + kinetic * force - decay * p  42.9 us
    ppermute x4, waiting for transfers between devices, neighbours(): lax.ppermute(plane, 'gz', [(i, (i + 1) % count) for i in range(count)])  33.1 us
    pallas_call x2, Pallas kernels, forward(): pl.pallas_call(functools.partial(forward_kernel, h), grid=(6,), in_specs=...  24.5 us
    pallas_call x2, Pallas kernels, inverse(): pl.pallas_call(functools.partial(inverse_kernel, h), grid=(6,), in_specs=...  23.5 us
    mul x1, other arithmetic, shards(): m2 = 2.0 * (scale * shear)  22.4 us
    all_to_all x6, starting transfers between devices, swap(): return lax.all_to_all(chunk, 'gz', split_axis=0, concat_axis=0, tiled=True)  20.3 us
  transfers between devices with their start and end apart: 14, of which 9 were waited for; matrix products, arithmetic and copies ran while one was open for 11% of the time, Pallas kernels for 6%

profile of v1, /device:TPU:0, one launch (start us, length us, event | category | flops | bytes accessed | tf_op | source)
XLA Modules:
  0.0 477.0 jit_solution(14294713369713982094)
XLA Ops:
  1.1 6.0 %collective-permute-start.1 = (f32[512,512]{1,0:T(8,128)}, f32[512,512]{1,0:T(8,128)S(1)}, u32[]{:S(2)}, u32[]{:S(2)}) collective-permute-start(f32[512,512]{1,0:T(8,128)} %bitcast.139), channel_id=1, source_target_pairs={{1,0},{2,1},{3,2},{4,3},{5,4},{6,5},{7,6},{8,7},{9,8},{10,9},{11,1... | collective-permute-start | bytes 3145736 | tf_op jit(solution)/shard_map/ppermute | solution.py:34
  7.1 5.3 %collective-permute-start.5 = (f32[512,512]{1,0:T(8,128)}, f32[512,512]{1,0:T(8,128)S(1)}, u32[]{:S(2)}, u32[]{:S(2)}) collective-permute-start(f32[512,512]{1,0:T(8,128)} %bitcast.143), channel_id=1, source_target_pairs={{1,0},{2,1},{3,2},{4,3},{5,4},{6,5},{7,6},{8,7},{9,8},{10,9},{11,1... | collective-permute-start | bytes 3145736 | tf_op jit(solution)/shard_map/ppermute | solution.py:34
  12.5 2.0 fusion.48
  14.7 1.0 copy-done.24
  19.9 1.0 slice-done
  20.9 0.7 slice-done.1
  22.2 42.9 %fusion.10 = (f32[512,512]{1,0:T(8,128)S(1)}, f32[512,512]{1,0:T(8,128)S(1)}, pred[1,512,512]{2,1,0:T(8,128)(4,1)S(1)}, pred[1,512,512]{2,1,0:T(8,128)(4,1)S(1)}...) fusion(f32[511,512]{1,0:T(8,128)S(1)} %get-tuple-element.68, ...), kind=kLoop, calls=%fused_computation.13 | loop fusion | flops 34340864 | bytes 23068896 | tf_op jit(solution)/shard_map/sub | solution.py:48
  65.2 16.1 %collective-permute-start.2 = (f32[512,512]{1,0:T(8,128)S(1)}, f32[512,512]{1,0:T(8,128)S(1)}, u32[]{:S(2)}, u32[]{:S(2)}) collective-permute-start(f32[512,512]{1,0:T(8,128)S(1)} %get-tuple-element.21), channel_id=1, source_target_pairs={{0,1},{1,2},{2,3},{3,4},{4,5},{5,6},{6,7},{7,8},{8,9},{9,10},{10,1... | collective-permute-start | bytes 3145736 | tf_op jit(solution)/shard_map/ppermute | solution.py:33
  82.1 1.5 collective-permute-done.2
  83.6 10.0 %collective-permute-done.3 = f32[512,512]{1,0:T(8,128)S(1)} collective-permute-done((f32[512,512]{1,0:T(8,128)S(1)}, f32[512,512]{1,0:T(8,128)S(1)}, u32[]{:S(2)}, u32[]{:S(2)}) %collective-permute-start.3) | collective-permute-done | bytes 1048608 | tf_op jit(solution)/shard_map/ppermute | solution.py:34
  93.6 1.0 copy-done.31
  94.6 22.4 %multiply_multiply_fusion.1 = (f32[512,512]{1,0:T(8,128)S(1)}, f32[512,512]{1,0:T(8,128)S(1)}, f32[512,512]{1,0:T(8,128)}) fusion(pred[1,512,512]{2,1,0:T(8,128)(4,1)S(1)} %get-tuple-element.38, pred[1,512,512]{2,1,0:T(8,128)(4,1)S(1)} %get-tuple-element.37, pred[1,512,512]{2,1,0:T(8,128)(4,1)S(1)} %get-tuple-element.36, ...), kind=kLoop, calls=%fused_computation.51 | loop fusion | flops 21233664 | bytes 25165920 | tf_op jit(solution)/shard_map/mul | solution.py:370
  117.0 12.2 %bitcast_multiply_fusion.3.lt_ref = f32[512,512]{1,0:T(8,128)S(1)} fusion(f32[6,1,512,512]{3,2,1,0:T(8,128)S(1)} %bitcast.150, f32[512,512]{1,0:T(8,128)S(1)} %get-tuple-element.19, pred[1,512,512]{2,1,0:T(8,128)(4,1)S(1)} %get-tuple-element.38, pred[1,512,512]{2,1,0:T(8,128)(4,1)S(1)} %get-tuple-element.37, pred[1,512,512]{2,1,0:T(8,128)(4,1)S(1)} %get-tuple-element.36, ...), kind=kLoop, calls=%fused_computation.46 | loop fusion | flops 6553600 | bytes 9437248 | tf_op jit(solution)/shard_map/mul | solution.py:369
  129.3 12.3 %shard_map.157 = (f32[32,10,8,128]{3,2,1,0:T(8,128)}, f32[32,10,8,128]{3,2,1,0:T(8,128)}) custom-call(f32[6,512,512]{2,1,0:T(8,128)} %bitcast.146, f32[512,512]{1,0:T(8,128)S(1)} %bitcast_multiply_fusion.3.lt_ref, f32[512,512]{1,0:T(8,128)S(1)} %get-tuple-element.18.m2_ref, bf16[256,256]{1,0:T(8,128)(2,1)S(1)} %copy-done.19, ...), custom_call_target="tpu_custom_call" | custom-call | flops 3623878656 | bytes 14680064 | tf_op jit(solution)/shard_map/pallas_call | solution.py:149
  141.5 51.9 %all_to_all.40.x_ref = f32[32,10,8,128]{3,2,1,0:T(8,128)} all-to-all(f32[32,10,8,128]{3,2,1,0:T(8,128)} %get-tuple-element.13), channel_id=1, replica_groups=mesh['gz'=32] {'gz'}, dimensions={0} | all-to-all | bytes 2621440 | tf_op jit(solution)/shard_map/all_to_all | solution.py:378
  193.4 3.0 all-to-all-start.6
  196.4 1.0 copy-done.12
  197.5 1.0 copy-done.14
  198.5 0.9 copy-done.18
  199.4 12.3 %shard_map.158 = (f32[32,10,8,128]{3,2,1,0:T(8,128)}, f32[32,10,8,128]{3,2,1,0:T(8,128)}) custom-call(f32[6,512,512]{2,1,0:T(8,128)} %bitcast.147, f32[512,512]{1,0:T(8,128)S(1)} %bitcast_multiply_fusion.3.lt_ref, f32[512,512]{1,0:T(8,128)S(1)} %get-tuple-element.18.m2_ref, bf16[256,256]{1,0:T(8,128)(2,1)S(1)} %copy-done.18, ...), custom_call_target="tpu_custom_call" | custom-call | flops 3623878656 | bytes 14680064 | tf_op jit(solution)/shard_map/pallas_call | solution.py:149
  211.7 16.4 %all-to-all-done.6.x_ref = f32[32,10,8,128]{3,2,1,0:T(8,128)S(1)} async-done(((f32[32,10,8,128]{3,2,1,0:T(8,128)}), f32[32,10,8,128]{3,2,1,0:T(8,128)S(1)}, u32[]{:S(2)}, u32[]{:S(2)}) %all-to-all-start.6) | async-done | bytes 1310752 | tf_op jit(solution)/shard_map/all_to_all | solution.py:378
  228.1 37.0 %all_to_all.41.x_ref = f32[32,10,8,128]{3,2,1,0:T(8,128)} all-to-all(f32[32,10,8,128]{3,2,1,0:T(8,128)} %get-tuple-element.11), channel_id=1, replica_groups=mesh['gz'=32] {'gz'}, dimensions={0} | all-to-all | bytes 2621440 | tf_op jit(solution)/shard_map/all_to_all | solution.py:378
  265.2 2.7 all-to-all-start.2
  267.9 1.3 copy-done.2
  269.2 1.5 shard_map.161
  270.8 1.0 copy-done.3
  271.8 27.9 %all-to-all-done.2.x_ref = f32[32,10,8,128]{3,2,1,0:T(8,128)S(1)} async-done(((f32[32,10,8,128]{3,2,1,0:T(8,128)}), f32[32,10,8,128]{3,2,1,0:T(8,128)S(1)}, u32[]{:S(2)}, u32[]{:S(2)}) %all-to-all-start.2) | async-done | bytes 1310752 | tf_op jit(solution)/shard_map/all_to_all | solution.py:378
  299.7 3.8 all-to-all-start.5
  303.6 1.5 shard_map.162
  305.1 1.1 copy-done.5
  306.2 29.5 %all-to-all-done.5.r0_ref = f32[32,10,8,128]{3,2,1,0:T(8,128)} async-done(((f32[32,10,8,128]{3,2,1,0:T(8,128)}), f32[32,10,8,128]{3,2,1,0:T(8,128)}, u32[]{:S(2)}, u32[]{:S(2)}) %all-to-all-start.5) | async-done | bytes 1310752 | tf_op jit(solution)/shard_map/all_to_all | solution.py:378
  335.7 3.7 all-to-all-start.7
  339.4 1.5 shard_map.159
  340.9 1.0 copy-done.4
  341.9 29.5 %all-to-all-done.7.r1_ref = f32[32,10,8,128]{3,2,1,0:T(8,128)} async-done(((f32[32,10,8,128]{3,2,1,0:T(8,128)}), f32[32,10,8,128]{3,2,1,0:T(8,128)}, u32[]{:S(2)}, u32[]{:S(2)}) %all-to-all-start.7) | async-done | bytes 1310752 | tf_op jit(solution)/shard_map/all_to_all | solution.py:378
  371.5 3.6 all-to-all-start.1
  375.1 1.5 shard_map.160
  376.6 1.1 copy-done
  377.6 29.6 %all-to-all-done.1.r0_ref = f32[32,10,8,128]{3,2,1,0:T(8,128)S(1)} async-done(((f32[32,10,8,128]{3,2,1,0:T(8,128)}), f32[32,10,8,128]{3,2,1,0:T(8,128)S(1)}, u32[]{:S(2)}, u32[]{:S(2)}) %all-to-all-start.1) | async-done | bytes 1310752 | tf_op jit(solution)/shard_map/all_to_all | solution.py:378
  407.2 3.6 all-to-all-start.3
  411.1 5.1 %collective-permute-start.7 = (f32[512,512]{1,0:T(8,128)}, f32[512,512]{1,0:T(8,128)S(1)}, u32[]{:S(2)}, u32[]{:S(2)}) collective-permute-start(f32[512,512]{1,0:T(8,128)} %get-tuple-element.10), channel_id=1, source_target_pairs={{1,0},{2,1},{3,2},{4,3},{5,4},{6,5},{7,6},{8,7},{9,8},{10,9},{11,1... | collective-permute-start | bytes 3145736 | tf_op jit(solution)/shard_map/ppermute | solution.py:34
  416.2 0.8 fusion.41
  416.9 1.2 fusion.39
  418.8 31.3 %collective-permute-done.6 = f32[512,512]{1,0:T(8,128)S(1)} collective-permute-done((f32[512,512]{1,0:T(8,128)}, f32[512,512]{1,0:T(8,128)S(1)}, u32[]{:S(2)}, u32[]{:S(2)}) %collective-permute-start.6) | collective-permute-done | bytes 1048608 | tf_op jit(solution)/shard_map/ppermute | solution.py:33
  450.1 2.2 fusion.31
  452.4 11.6 %shard_map.163.rest_0_ = f32[6,512,256]{2,1,0:T(8,128)} custom-call(f32[32,10,8,128]{3,2,1,0:T(8,128)} %all-to-all-done.5.r0_ref, f32[32,10,8,128]{3,2,1,0:T(8,128)} %all-to-all-done.7.r1_ref, bf16[256,256]{1,0:T(8,128)(2,1)S(1)} %copy-done.15, bf16[256,256]{1,0:T(8,128)(2,1)S(1)} %copy-done.16, bf16[2,512,256]{2,1,0:T(8,128)(2,1)S(1)} %copy-done.6, ...), custom_call_target="tpu_custom_call" | custom-call | flops 3623878656 | bytes 14680064 | tf_op jit(solution)/shard_map/pallas_call | solution.py:313
  464.0 1.0 copy-done.8
  465.0 12.0 %shard_map.164 = f32[6,512,512]{2,1,0:T(8,128)} custom-call(f32[32,10,8,128]{3,2,1,0:T(8,128)S(1)} %all-to-all-done.1.r0_ref, f32[32,10,8,128]{3,2,1,0:T(8,128)S(1)} %all-to-all-done.3.r1_ref, bf16[256,256]{1,0:T(8,128)(2,1)S(1)} %copy-done.9, bf16[256,256]{1,0:T(8,128)(2,1)S(1)} %copy-done.10, bf16[2,512,256]{2,1,0:T(8,128)(2,1)S(1)} %copy-done.6, ...), custom_call_target="tpu_custom_call" | custom-call | flops 3623878656 | bytes 14680064 | tf_op jit(solution)/shard_map/pallas_call | solution.py:313
  (93 shorter events, 7.3 us)
Async XLA Ops:
  0.6 19.2 %collective-permute-start = (f32[512,512]{1,0:T(8,128)}, f32[512,512]{1,0:T(8,128)S(1)}, u32[]{:S(2)}, u32[]{:S(2)}) collective-permute-start(f32[512,512]{1,0:T(8,128)} %bitcast.138), channel_id=1, source_target_pairs={{0,1},{1,2},{2,3},{3,4},{4,5},{5,6},{6,7},{7,8},{8,9},{9,10},{10,1... | collective-permute-start | bytes 3145736 | tf_op jit(solution)/shard_map/ppermute | solution.py:33
  1.1 18.7 %collective-permute-start.1 = (f32[512,512]{1,0:T(8,128)}, f32[512,512]{1,0:T(8,128)S(1)}, u32[]{:S(2)}, u32[]{:S(2)}) collective-permute-start(f32[512,512]{1,0:T(8,128)} %bitcast.139), channel_id=1, source_target_pairs={{1,0},{2,1},{3,2},{4,3},{5,4},{6,5},{7,6},{8,7},{9,8},{10,9},{11,1... | collective-permute-start | bytes 3145736 | tf_op jit(solution)/shard_map/ppermute | solution.py:34
  7.1 7.3 %copy-start.23 = (f32[1,512,512]{2,1,0:T(8,128)S(1)}, f32[1,512,512]{2,1,0:T(8,128)}, u32[]{:S(2)}) copy-start(f32[1,512,512]{2,1,0:T(8,128)} %param.14) | copy-start | bytes 3145732
  7.1 75.0 %collective-permute-start.4 = (f32[512,512]{1,0:T(8,128)}, f32[512,512]{1,0:T(8,128)S(1)}, u32[]{:S(2)}, u32[]{:S(2)}) collective-permute-start(f32[512,512]{1,0:T(8,128)} %bitcast.142), channel_id=1, source_target_pairs={{0,1},{1,2},{2,3},{3,4},{4,5},{5,6},{6,7},{7,8},{8,9},{9,10},{10,1... | collective-permute-start | bytes 3145736 | tf_op jit(solution)/shard_map/ppermute | solution.py:33
  7.1 75.0 %collective-permute-start.5 = (f32[512,512]{1,0:T(8,128)}, f32[512,512]{1,0:T(8,128)S(1)}, u32[]{:S(2)}, u32[]{:S(2)}) collective-permute-start(f32[512,512]{1,0:T(8,128)} %bitcast.143), channel_id=1, source_target_pairs={{1,0},{2,1},{3,2},{4,3},{5,4},{6,5},{7,6},{8,7},{9,8},{10,9},{11,1... | collective-permute-start | bytes 3145736 | tf_op jit(solution)/shard_map/ppermute | solution.py:34
  14.5 1.2 copy-start.24
  14.5 1.4 copy-start.33
  14.5 2.1 copy-start.32
  14.5 2.8 copy-start.34
  18.7 2.2 slice-start
  18.9 2.7 slice-start.1
  19.3 2.6 copy-start.28
  19.3 2.9 copy-start.29
  65.2 29.4 %copy-start.21 = (f32[512,512]{1,0:T(8,128)}, f32[512,512]{1,0:T(8,128)S(1)}, u32[]{:S(2)}) copy-start(f32[512,512]{1,0:T(8,128)S(1)} %get-tuple-element.21) | copy-start | bytes 3145732
  65.2 18.4 %collective-permute-start.2 = (f32[512,512]{1,0:T(8,128)S(1)}, f32[512,512]{1,0:T(8,128)S(1)}, u32[]{:S(2)}, u32[]{:S(2)}) collective-permute-start(f32[512,512]{1,0:T(8,128)S(1)} %get-tuple-element.21), channel_id=1, source_target_pairs={{0,1},{1,2},{2,3},{3,4},{4,5},{5,6},{6,7},{7,8},{8,9},{9,10},{10,1... | collective-permute-start | bytes 3145736 | tf_op jit(solution)/shard_map/ppermute | solution.py:33
  81.3 12.3 %collective-permute-start.3 = (f32[512,512]{1,0:T(8,128)S(1)}, f32[512,512]{1,0:T(8,128)S(1)}, u32[]{:S(2)}, u32[]{:S(2)}) collective-permute-start(f32[512,512]{1,0:T(8,128)S(1)} %get-tuple-element.21), channel_id=1, source_target_pairs={{1,0},{2,1},{3,2},{4,3},{5,4},{6,5},{7,6},{8,7},{9,8},{10,9},{11,1... | collective-permute-start | bytes 3145736 | tf_op jit(solution)/shard_map/ppermute | solution.py:34
  82.1 11.5 %copy-start.30 = (f32[512,512]{1,0:T(8,128)}, f32[512,512]{1,0:T(8,128)S(1)}, u32[]{:S(2)}) copy-start(f32[512,512]{1,0:T(8,128)S(1)} %collective-permute-done.5) | copy-start | bytes 3145732
  117.0 12.2 %copy-start.26 = (f32[512,512]{1,0:T(8,128)}, f32[512,512]{1,0:T(8,128)S(1)}, u32[]{:S(2)}) copy-start(f32[512,512]{1,0:T(8,128)S(1)} %get-tuple-element.19) | copy-start | bytes 3145732
  117.0 12.2 %copy-start.11 = (bf16[2,512,256]{2,1,0:T(8,128)(2,1)S(1)}, bf16[2,512,256]{2,1,0:T(8,128)(2,1)}, u32[]{:S(2)}) copy-start(bf16[2,512,256]{2,1,0:T(8,128)(2,1)} %constant.93.yh_ref) | copy-start | bytes 1572868
  117.0 12.2 %copy-start.13 = (bf16[2,512,256]{2,1,0:T(8,128)(2,1)S(1)}, bf16[2,512,256]{2,1,0:T(8,128)(2,1)}, u32[]{:S(2)}) copy-start(bf16[2,512,256]{2,1,0:T(8,128)(2,1)} %constant.96.yl_ref) | copy-start | bytes 1572868
  117.0 12.2 %copy-start.19 = (bf16[256,256]{1,0:T(8,128)(2,1)S(1)}, bf16[256,256]{1,0:T(8,128)(2,1)}, u32[]{:S(2)}) copy-start(bf16[256,256]{1,0:T(8,128)(2,1)} %constant.89.xh_ref) | copy-start | bytes 393220
  117.0 12.2 %copy-start.20 = (bf16[256,256]{1,0:T(8,128)(2,1)S(1)}, bf16[256,256]{1,0:T(8,128)(2,1)}, u32[]{:S(2)}) copy-start(bf16[256,256]{1,0:T(8,128)(2,1)} %constant.92.xl_ref) | copy-start | bytes 393220
  193.4 3.0 copy-start.17
  193.4 34.7 %all-to-all-start.6 = ((f32[32,10,8,128]{3,2,1,0:T(8,128)}), f32[32,10,8,128]{3,2,1,0:T(8,128)S(1)}, u32[]{:S(2)}, u32[]{:S(2)}) async-start(f32[32,10,8,128]{3,2,1,0:T(8,128)} %get-tuple-element.14), calls=%async_computation.6 | async-start | bytes 2621440 | tf_op jit(solution)/shard_map/all_to_all | solution.py:378
  196.4 1.0 copy-start.12
  265.2 34.6 %all-to-all-start.2 = ((f32[32,10,8,128]{3,2,1,0:T(8,128)}), f32[32,10,8,128]{3,2,1,0:T(8,128)S(1)}, u32[]{:S(2)}, u32[]{:S(2)}) async-start(f32[32,10,8,128]{3,2,1,0:T(8,128)} %get-tuple-element.12), calls=%async_computation.2 | async-start | bytes 2621440 | tf_op jit(solution)/shard_map/all_to_all | solution.py:378
  267.9 1.3 copy-start.2
  270.7 1.1 copy-start.3
  299.7 35.9 %all-to-all-start.5 = ((f32[32,10,8,128]{3,2,1,0:T(8,128)}), f32[32,10,8,128]{3,2,1,0:T(8,128)}, u32[]{:S(2)}, u32[]{:S(2)}) async-start(f32[32,10,8,128]{3,2,1,0:T(8,128)} %copy-done.3), calls=%async_computation.5 | async-start | bytes 2621440 | tf_op jit(solution)/shard_map/all_to_all | solution.py:378
  305.1 1.1 copy-start.5
  306.2 33.2 %copy-start.1 = (f32[32,10,8,128]{3,2,1,0:T(8,128)S(1)}, f32[32,10,8,128]{3,2,1,0:T(8,128)}, u32[]{:S(2)}) copy-start(f32[32,10,8,128]{3,2,1,0:T(8,128)} %all_to_all.41.x_ref) | copy-start | bytes 3932164
  335.7 35.8 %all-to-all-start.7 = ((f32[32,10,8,128]{3,2,1,0:T(8,128)}), f32[32,10,8,128]{3,2,1,0:T(8,128)}, u32[]{:S(2)}, u32[]{:S(2)}) async-start(f32[32,10,8,128]{3,2,1,0:T(8,128)} %copy-done.5), calls=%async_computation.7 | async-start | bytes 2621440 | tf_op jit(solution)/shard_map/all_to_all | solution.py:378
  340.9 1.1 copy-start.4
  371.5 35.7 %all-to-all-start.1 = ((f32[32,10,8,128]{3,2,1,0:T(8,128)}), f32[32,10,8,128]{3,2,1,0:T(8,128)S(1)}, u32[]{:S(2)}, u32[]{:S(2)}) async-start(f32[32,10,8,128]{3,2,1,0:T(8,128)} %copy-done.4), calls=%async_computation.1 | async-start | bytes 2621440 | tf_op jit(solution)/shard_map/all_to_all | solution.py:378
  376.6 1.1 copy-start
  407.2 56.8 %all-to-all-start.3 = ((f32[32,10,8,128]{3,2,1,0:T(8,128)}), f32[32,10,8,128]{3,2,1,0:T(8,128)S(1)}, u32[]{:S(2)}, u32[]{:S(2)}) async-start(f32[32,10,8,128]{3,2,1,0:T(8,128)} %copy-done), calls=%async_computation.3 | async-start | bytes 2621440 | tf_op jit(solution)/shard_map/all_to_all | solution.py:378
  410.8 7.3 %copy-start.25 = (f32[512,512]{1,0:T(8,128)S(1)}, f32[512,512]{1,0:T(8,128)}, u32[]{:S(2)}) copy-start(f32[512,512]{1,0:T(8,128)} %get-tuple-element.10) | copy-start | bytes 3145732
  410.8 39.3 %collective-permute-start.6 = (f32[512,512]{1,0:T(8,128)}, f32[512,512]{1,0:T(8,128)S(1)}, u32[]{:S(2)}, u32[]{:S(2)}) collective-permute-start(f32[512,512]{1,0:T(8,128)} %get-tuple-element.10), channel_id=1, source_target_pairs={{0,1},{1,2},{2,3},{3,4},{4,5},{5,6},{6,7},{7,8},{8,9},{9,10},{10,1... | collective-permute-start | bytes 3145736 | tf_op jit(solution)/shard_map/ppermute | solution.py:33
  411.1 39.0 %collective-permute-start.7 = (f32[512,512]{1,0:T(8,128)}, f32[512,512]{1,0:T(8,128)S(1)}, u32[]{:S(2)}, u32[]{:S(2)}) collective-permute-start(f32[512,512]{1,0:T(8,128)} %get-tuple-element.10), channel_id=1, source_target_pairs={{1,0},{2,1},{3,2},{4,3},{5,4},{6,5},{7,6},{8,7},{9,8},{10,9},{11,1... | collective-permute-start | bytes 3145736 | tf_op jit(solution)/shard_map/ppermute | solution.py:34
  418.5 31.6 %copy-start.22 = (f32[512,512]{1,0:T(8,128)S(1)}, f32[512,512]{1,0:T(8,128)}, u32[]{:S(2)}) copy-start(f32[512,512]{1,0:T(8,128)} %copy-done.21) | copy-start | bytes 3145732
  418.5 31.6 %copy-start.27 = (f32[512,512]{1,0:T(8,128)S(1)}, f32[512,512]{1,0:T(8,128)}, u32[]{:S(2)}) copy-start(f32[512,512]{1,0:T(8,128)} %copy-done.26) | copy-start | bytes 3145732
  450.1 2.3 copy-start.6
  450.1 2.3 copy-start.7
  450.1 2.3 copy-start.15
  450.1 2.3 copy-start.16
  452.4 11.6 %copy-start.9 = (bf16[256,256]{1,0:T(8,128)(2,1)S(1)}, bf16[256,256]{1,0:T(8,128)(2,1)}, u32[]{:S(2)}) copy-start(bf16[256,256]{1,0:T(8,128)(2,1)} %constant.101.xh_ref) | copy-start | bytes 393220
  452.4 11.6 %copy-start.10 = (bf16[256,256]{1,0:T(8,128)(2,1)S(1)}, bf16[256,256]{1,0:T(8,128)(2,1)}, u32[]{:S(2)}) copy-start(bf16[256,256]{1,0:T(8,128)(2,1)} %constant.104.xl_ref) | copy-start | bytes 393220
  464.0 1.0 copy-start.8
  (3 other events, 2.9 us)

commit v2 on v1

--- a/solution.py
+++ b/solution.py
@@ -21,31 +21,84 @@
 LIMIT = 50 * 1024 * 1024
 
 
-def lookup(labels, table, first):
-    out = jnp.zeros(labels.shape, F32)
-    for k in range(table.shape[0]):
-        out = jnp.where(labels == k + first, table[k], out)
-    return out
-
-
 def neighbours(plane):
     count = lax.axis_size("gz")
     below = lax.ppermute(plane, "gz", [(i, (i + 1) % count) for i in range(count)])
     above = lax.ppermute(plane, "gz", [((i + 1) % count, i) for i in range(count)])
-    return below + above
-
-
-def laplace(plane, z_sum):
-    y_sum = jnp.roll(plane, 1, 0) + jnp.roll(plane, -1, 0)
-    x_sum = jnp.roll(plane, 1, 1) + jnp.roll(plane, -1, 1)
-    return z_sum + y_sum + x_sum - 6.0 * plane
-
-
-def order_step(p, c, lap, kinetic, decay):
+    return below, above
+
+
+def laplace_plane(plane):
+    ny, nx = plane.shape
+    y_sum = pltpu.roll(plane, 1, 0) + pltpu.roll(plane, ny - 1, 0)
+    x_sum = pltpu.roll(plane, 1, 1) + pltpu.roll(plane, nx - 1, 1)
+    return y_sum + x_sum - 6.0 * plane
+
+
+def order_part(p, c, kinetic, decay):
     well = 2.0 * p * (1.0 - p) * (1.0 - 2.0 * p)
     interp = 6.0 * p * (1.0 - p)
-    force = lap - well + 2.0 * interp * (c - conc_eq)
+    force = laplace_plane(p) - well + 2.0 * interp * (c - conc_eq)
     return p + kinetic * force - decay * p
+
+
+def local_kernel(
+    moduli_ref, mobility_ref, rate_ref, p_ref, c_ref, e_ref, ids_ref, seeds_ref,
+    lt_ref, m2_ref, kin_ref, dec_ref, pa_ref, ca_ref,
+):
+    rows = 8
+
+    def body(k, carry):
+        at = pl.ds(pl.multiple_of(k * rows, rows), rows)
+        ids, seeds = ids_ref[at, :], seeds_ref[at, :]
+        lame = jnp.zeros(ids.shape, F32)
+        shear, mobility, rate = lame, lame, lame
+        for n in range(mobility_ref.shape[0]):
+            hit = ids == n
+            lame = jnp.where(hit, moduli_ref[0, n], lame)
+            shear = jnp.where(hit, moduli_ref[1, n], shear)
+            mobility = jnp.where(hit, mobility_ref[n], mobility)
+        for n in range(rate_ref.shape[0]):
+            rate = jnp.where(seeds == n + 1, rate_ref[n], rate)
+        e = [e_ref[n, at, :] for n in range(6)]
+        trace = e[0] + e[1] + e[2]
+        square = (
+            e[0] * e[0] + e[1] * e[1] + e[2] * e[2]
+            + 2.0 * (e[3] * e[3] + e[4] * e[4] + e[5] * e[5])
+        )
+        energy = 0.5 * lame * trace * trace + shear * square
+        kin_ref[at, :] = time_step * mobility * (1.0 + energy / (1.0 + energy))
+        dec_ref[at, :] = time_step * rate
+        lt_ref[at, :] = lame * trace
+        m2_ref[at, :] = 2.0 * shear
+        return carry
+
+    lax.fori_loop(0, p_ref.shape[0] // rows, body, 0)
+    p, c = p_ref[...], c_ref[...]
+    pa_ref[...] = order_part(p, c, kin_ref[...], dec_ref[...])
+    ca_ref[...] = c + time_step * laplace_plane(c) + p
+
+
+def second_kernel(p1_ref, ca_ref, cb_ref, cu_ref, kin_ref, dec_ref, c1_ref, pa_ref, cc_ref):
+    p1 = p1_ref[...]
+    c1_ref[...] = ca_ref[...] + time_step * (cb_ref[...] + cu_ref[...]) - p1
+    pa_ref[...] = order_part(p1, c1_ref[...], kin_ref[...], dec_ref[...])
+    c1 = c1_ref[...]
+    cc_ref[...] = c1 + time_step * laplace_plane(c1) + p1
+
+
+def planes_call(kernel, scalars, arrays, outs):
+    shape = arrays[0].shape
+    total = sum(v.size * 4 for v in arrays) + outs * 4 * arrays[0].size
+    return pl.pallas_call(
+        kernel,
+        in_specs=[pl.BlockSpec(memory_space=pltpu.SMEM)] * len(scalars)
+        + [pl.BlockSpec(memory_space=pltpu.VMEM)] * len(arrays),
+        out_specs=[pl.BlockSpec(memory_space=pltpu.VMEM)] * outs,
+        out_shape=[jax.ShapeDtypeStruct(shape, F32)] * outs,
+        compiler_params=pltpu.CompilerParams(vmem_limit_bytes=LIMIT),
+        cost_estimate=pl.CostEstimate(flops=100 * total, bytes_accessed=total, transcendentals=0),
+    )(*scalars, *arrays)
 
 
 def pair(table):
@@ -91,24 +144,38 @@
     return mx, my
 
 
-def forward_kernel(h, e_ref, lt_ref, m2_ref, xh_ref, xl_ref, yh_ref, yl_ref, o0_ref, o1_ref):
+def forward_kernel(h, e_ref, lt_ref, m2_ref, xh_ref, xl_ref, yh_ref, yl_ref, *rest):
     t = pl.program_id(0)
+    scale_ref = rest[-1]
+
+    @pl.when(t == 0)
+    def _():
+        if h == 0:
+            pa_ref, kin_ref, pb_ref, pu_ref, _, p_ref, _ = rest
+            p_ref[...] = pa_ref[...] + kin_ref[...] * (pb_ref[...] + pu_ref[...])
+        else:
+            p_ref = rest[0]
+        p = p_ref[...]
+        scale_ref[...] = p * p * (3.0 - 2.0 * p) + residual_stiff
+
+    o_ref = rest[4] if h == 0 else rest[1]
+    nd, _, band, _ = o_ref.shape
     ny, nx = lt_ref.shape
     hy, hx, lanes = ny // 2, nx // 2, nx // 4
     diag = jnp.where((t == 0) | (t == 2) | (t == 5), 1.0, 0.0).astype(F32)
-    s = m2_ref[...] * e_ref[0] + diag * lt_ref[...]
+    s = scale_ref[...] * (m2_ref[...] * e_ref[0] + diag * lt_ref[...])
     left, right = s[:, :hx], s[:, hx:]
     folded = left + right if h == 0 else left - right
     xs = dot3(split(folded), (xh_ref[...], xl_ref[...]))
-    for g, o_ref in enumerate((o0_ref, o1_ref)):
-        nd, _, band, _ = o_ref.shape
+    for g in range(2):
         ys = xs[:hy] + xs[hy:] if g == 0 else xs[:hy] - xs[hy:]
         d = dot3((yh_ref[g], yl_ref[g]), split(ys))
         re = d[:hy, :lanes] + d[hy:, lanes:]
         im = d[:hy, lanes:] - d[hy:, :lanes]
         mx, my = waves((h, g), ny, lanes)
 
-        def put(slot, a, b, add=False):
+        def put(slot, a, b, add=False, base=10 * g):
+            slot = slot + base
             a, b = a.reshape(nd, band, lanes), b.reshape(nd, band, lanes)
             if add:
                 a, b = a + o_ref[:, slot], b + o_ref[:, slot + 1]
@@ -138,9 +205,10 @@
     return pl.BlockSpec(shape, lambda t: (0,) * len(shape))
 
 
-def forward(h, strain, lt, m2, fx, fy, devices):
+def forward(h, strain, lt, m2, fx, fy, devices, more):
     ny, nx = lt.shape
-    shape = (devices, 10, ny // 2 // devices, nx // 4)
+    shape = (devices, 20, ny // 2 // devices, nx // 4)
+    shapes = [shape, (ny, nx)] if h == 0 else [shape]
 
     def comp(t):
         c = jnp.where(t == 1, 5, jnp.where(t == 2, 1, jnp.where(t >= 3, 7 - t, 0)))
@@ -150,16 +218,17 @@
         functools.partial(forward_kernel, h),
         grid=(6,),
         in_specs=[pl.BlockSpec((1, ny, nx), comp), whole((ny, nx)), whole((ny, nx))]
-        + [whole(v.shape) for v in fx + fy],
-        out_specs=[whole(shape)] * 2,
-        out_shape=[jax.ShapeDtypeStruct(shape, F32)] * 2,
+        + [whole(v.shape) for v in fx + fy + more],
+        out_specs=[whole(v) for v in shapes],
+        out_shape=[jax.ShapeDtypeStruct(v, F32) for v in shapes],
+        scratch_shapes=[pltpu.VMEM((ny, nx), F32)],
         compiler_params=pltpu.CompilerParams(vmem_limit_bytes=LIMIT),
         cost_estimate=pl.CostEstimate(
             flops=6 * 3 * 2 * (ny * nx * nx // 4 + ny * ny * nx // 2),
             bytes_accessed=14 * 1024 * 1024,
             transcendentals=0,
         ),
-    )(strain, lt, m2, *fx, *fy)
+    )(strain, lt, m2, *fx, *fy, *more)
 
 
 def fft(re, im, sign):
@@ -203,43 +272,45 @@
                 dst[k, 2 * c + 1] = im[k]
             return carry
 
-        lax.fori_loop(0, 5, body, 0)
+        lax.fori_loop(0, x_ref.shape[1] // 2, body, 0)
 
     transform(x_ref, v_ref, -1.0)
     mx = (2 * lax.broadcasted_iota(jnp.int32, (band, lanes), 1) + h).astype(F32)
-    my = my_ref[...]
-    flat = mx * mx + my * my
 
     def body(k, carry):
         mz = jnp.where(k < depth // 2, k, k - depth).astype(F32)
-        k2 = flat + mz * mz
-        live = k2 > 0.5
-        inv = jnp.where(live, 1.0 / jnp.where(live, k2, 1.0), 0.0)
-        for part in range(2):
-            wx, wy, txz, tyz, tzz = [v_ref[k, 2 * c + part] for c in range(5)]
-            vx = wx + mz * txz
-            vy = wy + mz * tyz
-            vz = mx * txz + my * tyz + mz * tzz
-            inner = (mx * vx + my * vy + mz * vz) * (coupling * inv)
-            ux = (vx - mx * inner) * inv
-            uy = (vy - my * inner) * inv
-            uz = (vz - mz * inner) * inv
-            v_ref[k, part] = ux
-            v_ref[k, 2 + part] = uy
-            v_ref[k, 4 + part] = 0.5 * (mx * uz + mz * ux)
-            v_ref[k, 6 + part] = 0.5 * (my * uz + mz * uy)
-            v_ref[k, 8 + part] = mz * uz
+        for g in range(2):
+            my = my_ref[g]
+            k2 = mx * mx + my * my + mz * mz
+            live = k2 > 0.5
+            inv = jnp.where(live, 1.0 / jnp.where(live, k2, 1.0), 0.0)
+            for part in range(2):
+                at = 10 * g + part
+                wx, wy, txz, tyz, tzz = [v_ref[k, at + 2 * c] for c in range(5)]
+                vx = wx + mz * txz
+                vy = wy + mz * tyz
+                vz = mx * txz + my * tyz + mz * tzz
+                inner = (mx * vx + my * vy + mz * vz) * (coupling * inv)
+                ux = (vx - mx * inner) * inv
+                uy = (vy - my * inner) * inv
+                uz = (vz - mz * inner) * inv
+                v_ref[k, at] = ux
+                v_ref[k, at + 2] = uy
+                v_ref[k, at + 4] = 0.5 * (mx * uz + mz * ux)
+                v_ref[k, at + 6] = 0.5 * (my * uz + mz * uy)
+                v_ref[k, at + 8] = mz * uz
         return carry
 
     lax.fori_loop(0, depth, body, 0)
     transform(v_ref, o_ref, 1.0)
 
 
-def green(h, g, chunk, ny):
+def green(h, chunk, ny):
     depth, _, band, lanes = chunk.shape
-    row = 2 * (lax.axis_index("gz") * band + jnp.arange(band, dtype=jnp.int32)) + g
+    row = 2 * (lax.axis_index("gz") * band + jnp.arange(band, dtype=jnp.int32))
+    row = row[None] + jnp.arange(2, dtype=jnp.int32)[:, None]
     my = jnp.where(row < ny // 2, row, row - ny).astype(F32)
-    my = jnp.broadcast_to(my[:, None], (band, lanes))
+    my = jnp.broadcast_to(my[:, :, None], (2, band, lanes))
     return pl.pallas_call(
         functools.partial(green_kernel, h),
         in_specs=[pl.BlockSpec(memory_space=pltpu.VMEM)] * 2,
@@ -253,16 +324,17 @@
     )(chunk, my)
 
 
-def inverse_kernel(h, r0_ref, r1_ref, xh_ref, xl_ref, yh_ref, yl_ref, *rest):
+def inverse_kernel(h, r_ref, xh_ref, xl_ref, yh_ref, yl_ref, *rest):
     g_ref = rest[-1]
     t = pl.program_id(0)
-    lanes = r0_ref.shape[3]
-    hy = r0_ref.shape[0] * r0_ref.shape[2]
+    lanes = r_ref.shape[3]
+    hy = r_ref.shape[0] * r_ref.shape[2]
     sums = []
-    for g, r_ref in enumerate((r0_ref, r1_ref)):
+    for g in range(2):
         mx, my = waves((h, g), 2 * hy, lanes)
 
-        def get(slot):
+        def get(slot, base=10 * g):
+            slot = slot + base
             return [r_ref[:, slot + part].reshape(hy, lanes) for part in range(2)]
 
         def put(a, b):
@@ -305,7 +377,7 @@
         o_ref[0, :, hx:] = e_ref[0, :, hx:] - (z0 - z)
 
 
-def inverse(h, r0, r1, ix, iy, ny, nx, extra=()):
+def inverse(h, r, ix, iy, ny, nx, extra=()):
     def plane(width):
         return pl.BlockSpec((1, ny, width), lambda t: (t, 0, 0))
 
@@ -313,7 +385,7 @@
     return pl.pallas_call(
         functools.partial(inverse_kernel, h),
         grid=(6,),
-        in_specs=[whole(v.shape) for v in (r0, r1) + ix + iy]
+        in_specs=[whole(v.shape) for v in (r,) + ix + iy]
         + [plane(v.shape[2]) for v in extra],
         out_specs=plane(width),
         out_shape=jax.ShapeDtypeStruct((6, ny, width), F32),
@@ -324,7 +396,7 @@
             bytes_accessed=14 * 1024 * 1024,
             transcendentals=0,
         ),
-    )(r0, r1, *ix, *iy, *extra)
+    )(r, *ix, *iy, *extra)
 
 
 def shards(
@@ -344,42 +416,35 @@
     fy, iy = pair(fy), pair(iy)
     strain = strain.reshape(6, ny, nx)
     p, c = order_param[0], concentration[0]
-    p_sum = neighbours(p)
-    c_sum = neighbours(c)
-    ids, seeds = grain_ids[0], seed_labels[0]
-    lame = lookup(ids, grain_moduli[0], 0)
-    shear = lookup(ids, grain_moduli[1], 0)
-    mobility = lookup(ids, grain_mobility, 0)
-    rate = lookup(seeds, seed_rate, 1)
-    trace = strain[0] + strain[1] + strain[2]
-    square = (
-        strain[0] * strain[0]
-        + strain[1] * strain[1]
-        + strain[2] * strain[2]
-        + 2.0 * (strain[3] * strain[3] + strain[4] * strain[4] + strain[5] * strain[5])
+    p_halo = neighbours(p)
+    c_halo = neighbours(c)
+    lt, m2, kinetic, decay, p_part, c_part = planes_call(
+        local_kernel,
+        (grain_moduli, grain_mobility, seed_rate),
+        (p, c, strain, grain_ids[0], seed_labels[0]),
+        6,
     )
-    energy = 0.5 * lame * trace * trace + shear * square
-    kinetic = time_step * mobility * (1.0 + energy / (1.0 + energy))
-    decay = time_step * rate
-    p1 = order_step(p, c, laplace(p, p_sum), kinetic, decay)
-    p1_sum = neighbours(p1)
-    c1 = c + time_step * laplace(c, c_sum) + (p - p1)
-    p2 = order_step(p1, c1, laplace(p1, p1_sum), kinetic, decay)
-    scale = p2 * p2 * (3.0 - 2.0 * p2) + residual_stiff
-    lt = scale * lame * trace
-    m2 = 2.0 * (scale * shear)
-
-    sent = [list(forward(h, strain, lt, m2, fx[h], fy, devices)) for h in range(2)]
-    c1_late, sent[0][0] = lax.optimization_barrier((c1, sent[0][0]))
-    c1_sum = neighbours(c1_late)
-    c2 = c1_late + time_step * laplace(c1_late, c1_sum) + (p1 - p2)
+    p1 = p_part + kinetic * (p_halo[0] + p_halo[1])
+    p1_halo = neighbours(p1)
+    c1, p2_part, c2_part = planes_call(
+        second_kernel, (), (p1, c_part, *c_halo, kinetic, decay), 3
+    )
 
     def swap(chunk):
         return lax.all_to_all(chunk, "gz", split_axis=0, concat_axis=0, tiled=True)
 
-    back = [[swap(green(h, g, swap(sent[h][g]), ny)) for g in range(2)] for h in range(2)]
-    z0 = inverse(0, back[0][0], back[0][1], ix[0], iy, ny, nx)
-    out = inverse(1, back[1][0], back[1][1], ix[1], iy, ny, nx, (z0, strain))
+    sent0, p2 = forward(0, strain, lt, m2, fx[0], fy, devices, (p2_part, kinetic, *p1_halo))
+    (sent1,) = forward(1, strain, lt, m2, fx[1], fy, devices, (p2,))
+    band0 = swap(sent0)
+    band0, c1 = lax.optimization_barrier((band0, c1))
+    c1_halo = neighbours(c1)
+    band1 = swap(sent1)
+    back0 = swap(green(0, band0, ny))
+    done1, c1_halo = lax.optimization_barrier((green(1, band1, ny), c1_halo))
+    c2 = c2_part + time_step * (c1_halo[0] + c1_halo[1]) - p2
+    back1 = swap(done1)
+    z0 = inverse(0, back0, ix[0], iy, ny, nx)
+    out = inverse(1, back1, ix[1], iy, ny, nx, (z0, strain))
     return (p2[None], c2[None], out[:, None])
 
 

time: 482 us -> 378 us (0.78)
  blocking collectives: 88.9 us -> 0 us
  other arithmetic: 79.8 us -> 5.89 us
  starting transfers between devices: 53.6 us -> 79.8 us
  waiting for transfers between devices: 176 us -> 201 us
  Pallas kernels: 54.1 us -> 77.1 us
  local copies, waits for them, and re-layouts: 23.4 us -> 13.3 us
    all_to_all x2 -> x0, blocking collectives: 88.9 us -> none  [swap(): return lax.all_to_all(chunk, 'gz', split_axis=0, concat_axis=0, tiled=True)]
    sub x1 -> x0, other arithmetic: 42.9 us -> none  [order_step(): return p + kinetic * force - decay * p]
    ppermute x4, waiting for transfers between devices: 10 us -> 44.9 us  [neighbours(): lax.ppermute(plane, 'gz', [((i + 1) % count, i) for i in range(count)])]
    mul x2 -> x1, other arithmetic: 34.6 us -> 0.01 us  [green(): row = 2 * (lax.axis_index('gz') * band + jnp.arange(band, dtype=jnp.int32))]
    ppermute x4, waiting for transfers between devices: 33.1 us -> 4.11 us  [neighbours(): lax.ppermute(plane, 'gz', [(i, (i + 1) % count) for i in range(count)])]
    all_to_all x6 -> x4, starting transfers between devices: 20.3 us -> 39.6 us  [swap(): return lax.all_to_all(chunk, 'gz', split_axis=0, concat_axis=0, tiled=True)]
    all_to_all x6 -> x4, waiting for transfers between devices: 133 us -> 152 us  [swap(): return lax.all_to_all(chunk, 'gz', split_axis=0, concat_axis=0, tiled=True)]
    pallas_call x0 -> x2, Pallas kernels: none -> 16.8 us  [planes_call(): pl.pallas_call(kernel, in_specs=[pl.BlockSpec(memory_space=pltpu.SMEM)] *...]
  transfers between devices with their start and end apart: 14 -> 12, of which waited for: 9 -> 6; matrix products, arithmetic and copies ran while one was open for 11% -> 2% of each run, Pallas kernels for 6% -> 13%
where the time goes in v2:
time: 378 us
  waiting for transfers between devices  201 us (53%)
  starting transfers between devices  79.8 us (21%)
  Pallas kernels  77.1 us (20%)
  local copies, waits for them, and re-layouts  13.3 us (4%)
  other arithmetic  5.89 us (2%)
    all_to_all x4, waiting for transfers between devices, swap(): return lax.all_to_all(chunk, 'gz', split_axis=0, concat_axis=0, tiled=True)  152 us
    ppermute x4, waiting for transfers between devices, neighbours(): lax.ppermute(plane, 'gz', [((i + 1) % count, i) for i in range(count)])  44.9 us
    all_to_all x4, starting transfers between devices, swap(): return lax.all_to_all(chunk, 'gz', split_axis=0, concat_axis=0, tiled=True)  39.6 us
    pallas_call x2, Pallas kernels, forward(): pl.pallas_call(functools.partial(forward_kernel, h), grid=(6,), in_specs=...  28 us
    ppermute x4, starting transfers between devices, neighbours(): lax.ppermute(plane, 'gz', [((i + 1) % count, i) for i in range(count)])  22.4 us
    pallas_call x2, Pallas kernels, inverse(): pl.pallas_call(functools.partial(inverse_kernel, h), grid=(6,), in_specs=...  21.8 us
    ppermute x4, starting transfers between devices, neighbours(): lax.ppermute(plane, 'gz', [(i, (i + 1) % count) for i in range(count)])  17.8 us
    pallas_call x2, Pallas kernels, planes_call(): pl.pallas_call(kernel, in_specs=[pl.BlockSpec(memory_space=pltpu.SMEM)] *...  16.8 us
  transfers between devices with their start and end apart: 12, of which 6 were waited for; matrix products, arithmetic and copies ran while one was open for 2% of the time, Pallas kernels for 13%

profile of v2, /device:TPU:0, one launch (start us, length us, event | category | flops | bytes accessed | tf_op | source)
XLA Modules:
  0.0 377.7 jit_solution(6489216929091457259)
XLA Ops:
  0.6 6.4 %collective-permute-start.1 = (f32[512,512]{1,0:T(8,128)}, f32[512,512]{1,0:T(8,128)S(1)}, u32[]{:S(2)}, u32[]{:S(2)}) collective-permute-start(f32[512,512]{1,0:T(8,128)} %bitcast.19), channel_id=1, source_target_pairs={{1,0},{2,1},{3,2},{4,3},{5,4},{6,5},{7,6},{8,7},{9,8},{10,9},{11,1... | collective-permute-start | bytes 3145736 | tf_op jit(solution)/shard_map/ppermute | solution.py:27
  7.1 5.3 %collective-permute-start.3 = (f32[512,512]{1,0:T(8,128)}, f32[512,512]{1,0:T(8,128)S(1)}, u32[]{:S(2)}, u32[]{:S(2)}) collective-permute-start(f32[512,512]{1,0:T(8,128)} %bitcast.22), channel_id=1, source_target_pairs={{1,0},{2,1},{3,2},{4,3},{5,4},{6,5},{7,6},{8,7},{9,8},{10,9},{11,1... | collective-permute-start | bytes 3145736 | tf_op jit(solution)/shard_map/ppermute | solution.py:27
  12.4 0.7 copy-done.15
  13.1 0.7 copy-done.16
  13.7 0.7 copy-done.17
  14.4 11.7 %shard_map.157 = (f32[512,512]{1,0:T(8,128)S(1)}, f32[512,512]{1,0:T(8,128)S(1)}, f32[512,512]{1,0:T(8,128)S(1)}, f32[512,512]{1,0:T(8,128)}, f32[512,512]{1,0:T(8,128)}, /*index=5*/f32[512,512]{1,0:T(8,128)}) custom-call(f32[2,16]{1,0:T(2,128)S(1)} %copy-done.15, f32[16]{0:T(128)S(1)} %copy-done.16, f32[8]{0:T(128)S(1)} %copy-done.17, f32[512,512]{1,0:T(8,128)} %bitcast.21, ...), custom_call_target="tpu_custom_call" | custom-call | flops 1677721600 | bytes 16777216 | tf_op jit(solution)/shard_map/pallas_call | solution.py:93
  26.1 2.1 multiply_add_fusion.p1_ref
  28.2 0.0 copy-start.24
  28.3 5.4 %collective-permute-start.5 = (f32[512,512]{1,0:T(8,128)S(1)}, f32[512,512]{1,0:T(8,128)S(1)}, u32[]{:S(2)}, u32[]{:S(2)}) collective-permute-start(f32[512,512]{1,0:T(8,128)S(1)} %multiply_add_fusion.p1_ref), channel_id=1, source_target_pairs={{1,0},{2,1},{3,2},{4,3},{5,4},{6,5},{7,6},{8,7},{9,8},{10,9},{11,1... | collective-permute-start | bytes 3145736 | tf_op jit(solution)/shard_map/ppermute | solution.py:27
  33.6 17.8 %collective-permute-start.4 = (f32[512,512]{1,0:T(8,128)S(1)}, f32[512,512]{1,0:T(8,128)S(1)}, u32[]{:S(2)}, u32[]{:S(2)}) collective-permute-start(f32[512,512]{1,0:T(8,128)S(1)} %multiply_add_fusion.p1_ref), channel_id=1, source_target_pairs={{0,1},{1,2},{2,3},{3,4},{4,5},{5,6},{6,7},{7,8},{8,9},{9,10},{10,1... | collective-permute-start | bytes 3145736 | tf_op jit(solution)/shard_map/ppermute | solution.py:26
  51.5 0.9 copy-done.26
  52.4 0.3 copy-done.27
  52.8 5.1 %shard_map.158 = (f32[512,512]{1,0:T(8,128)S(1)}, f32[512,512]{1,0:T(8,128)S(1)}, f32[512,512]{1,0:T(8,128)S(1)}) custom-call(f32[512,512]{1,0:T(8,128)} %copy-done.24, f32[512,512]{1,0:T(8,128)} %get-tuple-element.23.ca_ref, f32[512,512]{1,0:T(8,128)} %copy-done.27, f32[512,512]{1,0:T(8,128)} %copy-done.26, f32[512,512]{1,0:T(8,128)} %copy-done.1, ...), custom_call_target="tpu_custom_call" | custom-call | flops 943718400 | bytes 9437184 | tf_op jit(solution)/shard_map/pallas_call | solution.py:93
  57.8 1.1 copy-done.4
  58.9 1.0 copy-done.5
  59.9 1.0 copy-done.28
  60.9 0.3 copy-done.29
  61.2 14.9 %shard_map.159 = (f32[32,20,8,128]{3,2,1,0:T(8,128)}, f32[512,512]{1,0:T(8,128)}) custom-call(f32[6,512,512]{2,1,0:T(8,128)} %bitcast.12, f32[512,512]{1,0:T(8,128)S(1)} %get-tuple-element.19.lt_ref, f32[512,512]{1,0:T(8,128)S(1)} %get-tuple-element.20.m2_ref, bf16[256,256]{1,0:T(8,128)(2,1)S(1)} %copy-done.14, bf16[256,256]{1,0:T(8,128)(2,1)S(1)} %copy-done.13, ...), custom_call_target="tpu_custom_call" | custom-call | flops 3623878656 | bytes 14680064 | tf_op jit(solution)/shard_map/pallas_call | solution.py:217
  76.1 22.1 %all-to-all-start.1 = ((f32[32,20,8,128]{3,2,1,0:T(8,128)}), f32[32,20,8,128]{3,2,1,0:T(8,128)}, u32[]{:S(2)}, u32[]{:S(2)}) async-start(f32[32,20,8,128]{3,2,1,0:T(8,128)} %get-tuple-element.28), calls=%async_computation.1 | async-start | bytes 5242880 | tf_op jit(solution)/shard_map/all_to_all | solution.py:434
  98.2 13.1 %shard_map.160 = f32[32,20,8,128]{3,2,1,0:T(8,128)} custom-call(f32[6,512,512]{2,1,0:T(8,128)} %bitcast.13, f32[512,512]{1,0:T(8,128)S(1)} %get-tuple-element.19.lt_ref, f32[512,512]{1,0:T(8,128)S(1)} %get-tuple-element.20.m2_ref, bf16[256,256]{1,0:T(8,128)(2,1)S(1)} %copy-done.22, bf16[256,256]{1,0:T(8,128)(2,1)S(1)} %copy-done.21, ...), custom_call_target="tpu_custom_call" | custom-call | flops 3623878656 | bytes 14680064 | tf_op jit(solution)/shard_map/pallas_call | solution.py:217
  111.3 47.1 %all-to-all-done.1.x_ref = f32[32,20,8,128]{3,2,1,0:T(8,128)} async-done(((f32[32,20,8,128]{3,2,1,0:T(8,128)}), f32[32,20,8,128]{3,2,1,0:T(8,128)}, u32[]{:S(2)}, u32[]{:S(2)}) %all-to-all-start.1) | async-done | bytes 2621472 | tf_op jit(solution)/shard_map/all_to_all | solution.py:434
  158.3 4.0 %all-to-all-start = ((f32[32,20,8,128]{3,2,1,0:T(8,128)}), f32[32,20,8,128]{3,2,1,0:T(8,128)S(1)}, u32[]{:S(2)}, u32[]{:S(2)}) async-start(f32[32,20,8,128]{3,2,1,0:T(8,128)} %shard_map.160), calls=%async_computation | async-start | bytes 5242880 | tf_op jit(solution)/shard_map/all_to_all | solution.py:434
  162.4 0.1 broadcast_in_dim.9.my_ref
  162.4 6.0 %shard_map.162 = f32[32,20,8,128]{3,2,1,0:T(8,128)} custom-call(f32[32,20,8,128]{3,2,1,0:T(8,128)} %all-to-all-done.1.x_ref, f32[2,8,128]{2,1,0:T(8,128)S(1)} %broadcast_in_dim.9.my_ref), custom_call_target="tpu_custom_call" | custom-call | flops 41943040 | bytes 5242880 | tf_op jit(solution)/shard_map/pallas_call | solution.py:314
  168.5 54.0 %all-to-all-done.x_ref = f32[32,20,8,128]{3,2,1,0:T(8,128)S(1)} async-done(((f32[32,20,8,128]{3,2,1,0:T(8,128)}), f32[32,20,8,128]{3,2,1,0:T(8,128)S(1)}, u32[]{:S(2)}, u32[]{:S(2)}) %all-to-all-start) | async-done | bytes 2621472 | tf_op jit(solution)/shard_map/all_to_all | solution.py:434
  222.5 1.5 copy-done.23
  224.0 4.0 %all-to-all-start.3 = ((f32[32,20,8,128]{3,2,1,0:T(8,128)}), f32[32,20,8,128]{3,2,1,0:T(8,128)S(1)}, u32[]{:S(2)}, u32[]{:S(2)}) async-start(f32[32,20,8,128]{3,2,1,0:T(8,128)} %shard_map.162), calls=%async_computation.3 | async-start | bytes 5242880 | tf_op jit(solution)/shard_map/all_to_all | solution.py:434
  228.0 5.3 %collective-permute-start.7 = (f32[512,512]{1,0:T(8,128)}, f32[512,512]{1,0:T(8,128)S(1)}, u32[]{:S(2)}, u32[]{:S(2)}) collective-permute-start(f32[512,512]{1,0:T(8,128)} %copy-done.18), channel_id=1, source_target_pairs={{1,0},{2,1},{3,2},{4,3},{5,4},{6,5},{7,6},{8,7},{9,8},{10,9},{11,1... | collective-permute-start | bytes 3145736 | tf_op jit(solution)/shard_map/ppermute | solution.py:27
  233.3 4.5 %shard_map.161 = f32[32,20,8,128]{3,2,1,0:T(8,128)S(1)} custom-call(f32[32,20,8,128]{3,2,1,0:T(8,128)} %copy-done.23, f32[2,8,128]{2,1,0:T(8,128)S(1)} %broadcast_in_dim.9.my_ref), custom_call_target="tpu_custom_call" | custom-call | flops 41943040 | bytes 5242880 | tf_op jit(solution)/shard_map/pallas_call | solution.py:314
  237.8 0.0 copy-start
  237.8 1.5 copy-done
  239.3 44.9 %collective-permute-done.7 = f32[512,512]{1,0:T(8,128)S(1)} collective-permute-done((f32[512,512]{1,0:T(8,128)}, f32[512,512]{1,0:T(8,128)S(1)}, u32[]{:S(2)}, u32[]{:S(2)}) %collective-permute-start.7) | collective-permute-done | bytes 1048608 | tf_op jit(solution)/shard_map/ppermute | solution.py:27
  284.2 1.0 copy-done.25
  285.2 4.1 %collective-permute-done.6 = f32[512,512]{1,0:T(8,128)} collective-permute-done((f32[512,512]{1,0:T(8,128)}, f32[512,512]{1,0:T(8,128)}, u32[]{:S(2)}, u32[]{:S(2)}) %collective-permute-start.6) | collective-permute-done | bytes 1048608 | tf_op jit(solution)/shard_map/ppermute | solution.py:26
  289.3 4.2 %all-to-all-done.3.r_ref = f32[32,20,8,128]{3,2,1,0:T(8,128)S(1)} async-done(((f32[32,20,8,128]{3,2,1,0:T(8,128)}), f32[32,20,8,128]{3,2,1,0:T(8,128)S(1)}, u32[]{:S(2)}, u32[]{:S(2)}) %all-to-all-start.3) | async-done | bytes 2621472 | tf_op jit(solution)/shard_map/all_to_all | solution.py:434
  293.5 1.5 copy-done.2
  295.0 9.5 %all-to-all-start.2 = ((f32[32,20,8,128]{3,2,1,0:T(8,128)}), f32[32,20,8,128]{3,2,1,0:T(8,128)S(1)}, u32[]{:S(2)}, u32[]{:S(2)}) async-start(f32[32,20,8,128]{3,2,1,0:T(8,128)} %copy-done), calls=%async_computation.2 | async-start | bytes 5242880 | tf_op jit(solution)/shard_map/all_to_all | solution.py:434
  304.5 0.0 copy-start.6
  304.6 0.0 copy-start.7
  304.6 0.0 copy-start.19
  304.6 0.0 copy-start.20
  304.6 3.8 %subtract_bitcast_fusion = f32[1,512,512]{2,1,0:T(8,128)} fusion(f32[512,512]{1,0:T(8,128)} %get-tuple-element.26.rest_0_, f32[512,512]{1,0:T(8,128)} %copy-done.4, f32[512,512]{1,0:T(8,128)} %collective-permute-done.6, f32[512,512]{1,0:T(8,128)} %copy-done.25), kind=kLoop, calls=%fused_computation | loop fusion | flops 1048576 | bytes 5242880 | tf_op jit(solution)/shard_map/broadcast_in_dim | solution.py:448
  308.4 0.0 copy-start.11
  308.4 0.0 copy-start.12
  308.4 9.8 %shard_map.163.rest_0_ = f32[6,512,256]{2,1,0:T(8,128)} custom-call(f32[32,20,8,128]{3,2,1,0:T(8,128)S(1)} %copy-done.3, bf16[256,256]{1,0:T(8,128)(2,1)S(1)} %copy-done.20, bf16[256,256]{1,0:T(8,128)(2,1)S(1)} %copy-done.19, bf16[2,512,256]{2,1,0:T(8,128)(2,1)S(1)} %copy-done.7, bf16[2,512,256]{2,1,0:T(8,128)(2,1)S(1)} %copy-done.6), custom_call_target="tpu_custom_call" | custom-call | flops 3623878656 | bytes 14680064 | tf_op jit(solution)/shard_map/pallas_call | solution.py:385
  318.2 46.4 %all-to-all-done.2.r_ref = f32[32,20,8,128]{3,2,1,0:T(8,128)S(1)} async-done(((f32[32,20,8,128]{3,2,1,0:T(8,128)}), f32[32,20,8,128]{3,2,1,0:T(8,128)S(1)}, u32[]{:S(2)}, u32[]{:S(2)}) %all-to-all-start.2) | async-done | bytes 2621472 | tf_op jit(solution)/shard_map/all_to_all | solution.py:434
  364.6 1.0 copy-done.8
  365.7 12.0 %shard_map.164 = f32[6,512,512]{2,1,0:T(8,128)} custom-call(f32[32,20,8,128]{3,2,1,0:T(8,128)S(1)} %all-to-all-done.2.r_ref, bf16[256,256]{1,0:T(8,128)(2,1)S(1)} %copy-done.12, bf16[256,256]{1,0:T(8,128)(2,1)S(1)} %copy-done.11, bf16[2,512,256]{2,1,0:T(8,128)(2,1)S(1)} %copy-done.8, bf16[2,512,256]{2,1,0:T(8,128)(2,1)S(1)} %copy-done.6, ...), custom_call_target="tpu_custom_call" | custom-call | flops 3623878656 | bytes 14680064 | tf_op jit(solution)/shard_map/pallas_call | solution.py:385
  (49 shorter events, 0.1 us)
Async XLA Ops:
  0.6 25.5 %collective-permute-start.1 = (f32[512,512]{1,0:T(8,128)}, f32[512,512]{1,0:T(8,128)S(1)}, u32[]{:S(2)}, u32[]{:S(2)}) collective-permute-start(f32[512,512]{1,0:T(8,128)} %bitcast.19), channel_id=1, source_target_pairs={{1,0},{2,1},{3,2},{4,3},{5,4},{6,5},{7,6},{8,7},{9,8},{10,9},{11,1... | collective-permute-start | bytes 3145736 | tf_op jit(solution)/shard_map/ppermute | solution.py:27
  7.1 19.1 %collective-permute-start = (f32[512,512]{1,0:T(8,128)}, f32[512,512]{1,0:T(8,128)S(1)}, u32[]{:S(2)}, u32[]{:S(2)}) collective-permute-start(f32[512,512]{1,0:T(8,128)} %bitcast.20), channel_id=1, source_target_pairs={{0,1},{1,2},{2,3},{3,4},{4,5},{5,6},{6,7},{7,8},{8,9},{9,10},{10,1... | collective-permute-start | bytes 3145736 | tf_op jit(solution)/shard_map/ppermute | solution.py:26
  7.1 44.4 %collective-permute-start.3 = (f32[512,512]{1,0:T(8,128)}, f32[512,512]{1,0:T(8,128)S(1)}, u32[]{:S(2)}, u32[]{:S(2)}) collective-permute-start(f32[512,512]{1,0:T(8,128)} %bitcast.22), channel_id=1, source_target_pairs={{1,0},{2,1},{3,2},{4,3},{5,4},{6,5},{7,6},{8,7},{9,8},{10,9},{11,1... | collective-permute-start | bytes 3145736 | tf_op jit(solution)/shard_map/ppermute | solution.py:27
  12.4 39.0 %collective-permute-start.2 = (f32[512,512]{1,0:T(8,128)}, f32[512,512]{1,0:T(8,128)S(1)}, u32[]{:S(2)}, u32[]{:S(2)}) collective-permute-start(f32[512,512]{1,0:T(8,128)} %bitcast.23), channel_id=1, source_target_pairs={{0,1},{1,2},{2,3},{3,4},{4,5},{5,6},{6,7},{7,8},{8,9},{9,10},{10,1... | collective-permute-start | bytes 3145736 | tf_op jit(solution)/shard_map/ppermute | solution.py:26
  12.4 0.7 copy-start.15
  13.1 0.7 copy-start.16
  13.7 0.7 copy-start.17
  26.1 2.1 copy-start.1
  28.2 23.2 %copy-start.24 = (f32[512,512]{1,0:T(8,128)}, f32[512,512]{1,0:T(8,128)S(1)}, u32[]{:S(2)}) copy-start(f32[512,512]{1,0:T(8,128)S(1)} %multiply_add_fusion.p1_ref) | copy-start | bytes 3145732
  28.3 31.6 %collective-permute-start.5 = (f32[512,512]{1,0:T(8,128)S(1)}, f32[512,512]{1,0:T(8,128)S(1)}, u32[]{:S(2)}, u32[]{:S(2)}) collective-permute-start(f32[512,512]{1,0:T(8,128)S(1)} %multiply_add_fusion.p1_ref), channel_id=1, source_target_pairs={{1,0},{2,1},{3,2},{4,3},{5,4},{6,5},{7,6},{8,7},{9,8},{10,9},{11,1... | collective-permute-start | bytes 3145736 | tf_op jit(solution)/shard_map/ppermute | solution.py:27
  33.6 26.2 %collective-permute-start.4 = (f32[512,512]{1,0:T(8,128)S(1)}, f32[512,512]{1,0:T(8,128)S(1)}, u32[]{:S(2)}, u32[]{:S(2)}) collective-permute-start(f32[512,512]{1,0:T(8,128)S(1)} %multiply_add_fusion.p1_ref), channel_id=1, source_target_pairs={{0,1},{1,2},{2,3},{3,4},{4,5},{5,6},{6,7},{7,8},{8,9},{9,10},{10,1... | collective-permute-start | bytes 3145736 | tf_op jit(solution)/shard_map/ppermute | solution.py:26
  51.4 1.0 copy-start.26
  51.4 1.3 copy-start.27
  52.7 8.5 %copy-start.9 = (bf16[2,512,256]{2,1,0:T(8,128)(2,1)S(1)}, bf16[2,512,256]{2,1,0:T(8,128)(2,1)}, u32[]{:S(2)}) copy-start(bf16[2,512,256]{2,1,0:T(8,128)(2,1)} %constant.45.yl_ref) | copy-start | bytes 1572868
  52.7 8.5 %copy-start.10 = (bf16[2,512,256]{2,1,0:T(8,128)(2,1)S(1)}, bf16[2,512,256]{2,1,0:T(8,128)(2,1)}, u32[]{:S(2)}) copy-start(bf16[2,512,256]{2,1,0:T(8,128)(2,1)} %constant.42.yh_ref) | copy-start | bytes 1572868
  52.7 8.5 %copy-start.13 = (bf16[256,256]{1,0:T(8,128)(2,1)S(1)}, bf16[256,256]{1,0:T(8,128)(2,1)}, u32[]{:S(2)}) copy-start(bf16[256,256]{1,0:T(8,128)(2,1)} %constant.41.xl_ref) | copy-start | bytes 393220
  52.7 8.5 %copy-start.14 = (bf16[256,256]{1,0:T(8,128)(2,1)S(1)}, bf16[256,256]{1,0:T(8,128)(2,1)}, u32[]{:S(2)}) copy-start(bf16[256,256]{1,0:T(8,128)(2,1)} %constant.38.xh_ref) | copy-start | bytes 393220
  57.8 1.1 copy-start.4
  58.9 1.0 copy-start.5
  59.8 16.3 %copy-start.18 = (f32[512,512]{1,0:T(8,128)}, f32[512,512]{1,0:T(8,128)S(1)}, u32[]{:S(2)}) copy-start(f32[512,512]{1,0:T(8,128)S(1)} %get-tuple-element.30) | copy-start | bytes 3145732
  59.9 1.0 copy-start.28
  59.9 1.3 copy-start.29
  76.1 22.1 %copy-start.21 = (bf16[256,256]{1,0:T(8,128)(2,1)S(1)}, bf16[256,256]{1,0:T(8,128)(2,1)}, u32[]{:S(2)}) copy-start(bf16[256,256]{1,0:T(8,128)(2,1)} %constant.49.xl_ref) | copy-start | bytes 393220
  76.1 22.1 %copy-start.22 = (bf16[256,256]{1,0:T(8,128)(2,1)S(1)}, bf16[256,256]{1,0:T(8,128)(2,1)}, u32[]{:S(2)}) copy-start(bf16[256,256]{1,0:T(8,128)(2,1)} %constant.46.xh_ref) | copy-start | bytes 393220
  76.1 82.2 %all-to-all-start.1 = ((f32[32,20,8,128]{3,2,1,0:T(8,128)}), f32[32,20,8,128]{3,2,1,0:T(8,128)}, u32[]{:S(2)}, u32[]{:S(2)}) async-start(f32[32,20,8,128]{3,2,1,0:T(8,128)} %get-tuple-element.28), calls=%async_computation.1 | async-start | bytes 5242880 | tf_op jit(solution)/shard_map/all_to_all | solution.py:434
  158.3 64.2 %all-to-all-start = ((f32[32,20,8,128]{3,2,1,0:T(8,128)}), f32[32,20,8,128]{3,2,1,0:T(8,128)S(1)}, u32[]{:S(2)}, u32[]{:S(2)}) async-start(f32[32,20,8,128]{3,2,1,0:T(8,128)} %shard_map.160), calls=%async_computation | async-start | bytes 5242880 | tf_op jit(solution)/shard_map/all_to_all | solution.py:434
  222.5 1.5 copy-start.23
  224.0 69.5 %all-to-all-start.3 = ((f32[32,20,8,128]{3,2,1,0:T(8,128)}), f32[32,20,8,128]{3,2,1,0:T(8,128)S(1)}, u32[]{:S(2)}, u32[]{:S(2)}) async-start(f32[32,20,8,128]{3,2,1,0:T(8,128)} %shard_map.162), calls=%async_computation.3 | async-start | bytes 5242880 | tf_op jit(solution)/shard_map/all_to_all | solution.py:434
  228.0 56.2 %collective-permute-start.7 = (f32[512,512]{1,0:T(8,128)}, f32[512,512]{1,0:T(8,128)S(1)}, u32[]{:S(2)}, u32[]{:S(2)}) collective-permute-start(f32[512,512]{1,0:T(8,128)} %copy-done.18), channel_id=1, source_target_pairs={{1,0},{2,1},{3,2},{4,3},{5,4},{6,5},{7,6},{8,7},{9,8},{10,9},{11,1... | collective-permute-start | bytes 3145736 | tf_op jit(solution)/shard_map/ppermute | solution.py:27
  233.3 56.0 %collective-permute-start.6 = (f32[512,512]{1,0:T(8,128)}, f32[512,512]{1,0:T(8,128)}, u32[]{:S(2)}, u32[]{:S(2)}) collective-permute-start(f32[512,512]{1,0:T(8,128)} %copy-done.18), channel_id=1, source_target_pairs={{0,1},{1,2},{2,3},{3,4},{4,5},{5,6},{6,7},{7,8},{8,9},{9,10},{10,1... | collective-permute-start | bytes 3145736 | tf_op jit(solution)/shard_map/ppermute | solution.py:26
  237.8 1.5 copy-start
  284.2 1.0 copy-start.25
  293.5 1.5 copy-start.2
  295.0 69.6 %all-to-all-start.2 = ((f32[32,20,8,128]{3,2,1,0:T(8,128)}), f32[32,20,8,128]{3,2,1,0:T(8,128)S(1)}, u32[]{:S(2)}, u32[]{:S(2)}) async-start(f32[32,20,8,128]{3,2,1,0:T(8,128)} %copy-done), calls=%async_computation.2 | async-start | bytes 5242880 | tf_op jit(solution)/shard_map/all_to_all | solution.py:434
  304.5 3.8 %copy-start.3 = (f32[32,20,8,128]{3,2,1,0:T(8,128)S(1)}, f32[32,20,8,128]{3,2,1,0:T(8,128)}, u32[]{:S(2)}) copy-start(f32[32,20,8,128]{3,2,1,0:T(8,128)} %copy-done.2) | copy-start | bytes 7864324
  304.5 3.8 %copy-start.6 = (bf16[2,512,256]{2,1,0:T(8,128)(2,1)S(1)}, bf16[2,512,256]{2,1,0:T(8,128)(2,1)}, u32[]{:S(2)}) copy-start(bf16[2,512,256]{2,1,0:T(8,128)(2,1)} %constant.57.yl_ref) | copy-start | bytes 1572868
  304.6 3.8 %copy-start.7 = (bf16[2,512,256]{2,1,0:T(8,128)(2,1)S(1)}, bf16[2,512,256]{2,1,0:T(8,128)(2,1)}, u32[]{:S(2)}) copy-start(bf16[2,512,256]{2,1,0:T(8,128)(2,1)} %constant.54.yh_ref) | copy-start | bytes 1572868
  304.6 3.8 %copy-start.19 = (bf16[256,256]{1,0:T(8,128)(2,1)S(1)}, bf16[256,256]{1,0:T(8,128)(2,1)}, u32[]{:S(2)}) copy-start(bf16[256,256]{1,0:T(8,128)(2,1)} %constant.61.xl_ref) | copy-start | bytes 393220
  304.6 3.8 %copy-start.20 = (bf16[256,256]{1,0:T(8,128)(2,1)S(1)}, bf16[256,256]{1,0:T(8,128)(2,1)}, u32[]{:S(2)}) copy-start(bf16[256,256]{1,0:T(8,128)(2,1)} %constant.58.xh_ref) | copy-start | bytes 393220
  308.4 56.2 %copy-start.11 = (bf16[256,256]{1,0:T(8,128)(2,1)S(1)}, bf16[256,256]{1,0:T(8,128)(2,1)}, u32[]{:S(2)}) copy-start(bf16[256,256]{1,0:T(8,128)(2,1)} %constant.53.xl_ref) | copy-start | bytes 393220
  308.4 56.2 %copy-start.12 = (bf16[256,256]{1,0:T(8,128)(2,1)S(1)}, bf16[256,256]{1,0:T(8,128)(2,1)}, u32[]{:S(2)}) copy-start(bf16[256,256]{1,0:T(8,128)(2,1)} %constant.50.xh_ref) | copy-start | bytes 393220
  364.6 1.0 copy-start.8

commit v3 on v2

--- a/solution.py
+++ b/solution.py
@@ -3,6 +3,7 @@
 
 import jax
 import jax.numpy as jnp
+import ml_dtypes
 import numpy as np
 from jax import lax
 from jax.experimental import pallas as pl
@@ -101,10 +102,11 @@
     )(*scalars, *arrays)
 
 
-def pair(table):
-    table = jnp.asarray(np.asarray(table, np.float32))
-    hi = table.astype(BF16)
-    return hi, (table - hi.astype(F32)).astype(BF16)
+def triple(table, axis, order):
+    table = np.asarray(table, np.float32)
+    hi = table.astype(ml_dtypes.bfloat16)
+    lo = (table - hi.astype(np.float32)).astype(ml_dtypes.bfloat16)
+    return jnp.asarray(np.concatenate([(hi, lo)[k] for k in order], axis=axis))
 
 
 def tables(nx, ny, depth):
@@ -130,11 +132,16 @@
     return hi, (x - hi.astype(F32)).astype(BF16)
 
 
-def dot3(a, b):
-    def dot(u, v):
-        return jnp.dot(u, v, preferred_element_type=F32)
-
-    return dot(a[0], b[0]) + (dot(a[0], b[1]) + dot(a[1], b[0]))
+def dot_right(a, table):
+    hi, lo = split(a)
+    left = jnp.concatenate([hi, hi, lo], axis=1)
+    return jnp.dot(left, table, preferred_element_type=F32)
+
+
+def dot_left(table, b):
+    hi, lo = split(b)
+    right = jnp.concatenate([hi, hi, lo], axis=0)
+    return jnp.dot(table, right, preferred_element_type=F32)
 
 
 def waves(par, ny, lanes):
@@ -144,7 +151,7 @@
     return mx, my
 
 
-def forward_kernel(h, e_ref, lt_ref, m2_ref, xh_ref, xl_ref, yh_ref, yl_ref, *rest):
+def forward_kernel(h, e_ref, lt_ref, m2_ref, x_ref, y_ref, *rest):
     t = pl.program_id(0)
     scale_ref = rest[-1]
 
@@ -166,10 +173,10 @@
     s = scale_ref[...] * (m2_ref[...] * e_ref[0] + diag * lt_ref[...])
     left, right = s[:, :hx], s[:, hx:]
     folded = left + right if h == 0 else left - right
-    xs = dot3(split(folded), (xh_ref[...], xl_ref[...]))
+    xs = dot_right(folded, x_ref[...])
     for g in range(2):
         ys = xs[:hy] + xs[hy:] if g == 0 else xs[:hy] - xs[hy:]
-        d = dot3((yh_ref[g], yl_ref[g]), split(ys))
+        d = dot_left(y_ref[g], ys)
         re = d[:hy, :lanes] + d[hy:, lanes:]
         im = d[:hy, lanes:] - d[hy:, :lanes]
         mx, my = waves((h, g), ny, lanes)
@@ -218,7 +225,7 @@
         functools.partial(forward_kernel, h),
         grid=(6,),
         in_specs=[pl.BlockSpec((1, ny, nx), comp), whole((ny, nx)), whole((ny, nx))]
-        + [whole(v.shape) for v in fx + fy + more],
+        + [whole(v.shape) for v in (fx, fy) + more],
         out_specs=[whole(v) for v in shapes],
         out_shape=[jax.ShapeDtypeStruct(v, F32) for v in shapes],
         scratch_shapes=[pltpu.VMEM((ny, nx), F32)],
@@ -228,7 +235,7 @@
             bytes_accessed=14 * 1024 * 1024,
             transcendentals=0,
         ),
-    )(strain, lt, m2, *fx, *fy, *more)
+    )(strain, lt, m2, fx, fy, *more)
 
 
 def fft(re, im, sign):
@@ -324,7 +331,7 @@
     )(chunk, my)
 
 
-def inverse_kernel(h, r_ref, xh_ref, xl_ref, yh_ref, yl_ref, *rest):
+def inverse_kernel(h, r_ref, x_ref, y_ref, *rest):
     g_ref = rest[-1]
     t = pl.program_id(0)
     lanes = r_ref.shape[3]
@@ -361,12 +368,12 @@
         def _():
             put(*get(2 * (6 - t)))
 
-        d = dot3((yh_ref[g], yl_ref[g]), split(g_ref[...]))
+        d = dot_left(y_ref[g], g_ref[...])
         re = d[:hy, :lanes] - d[hy:, lanes:]
         im = d[:hy, lanes:] + d[hy:, :lanes]
         sums.append(jnp.concatenate([re, im], axis=1))
     full = jnp.concatenate([sums[0] + sums[1], sums[0] - sums[1]], axis=0)
-    z = dot3(split(full), (xh_ref[...], xl_ref[...]))
+    z = dot_right(full, x_ref[...])
     if h == 0:
         rest[0][0] = z
     else:
@@ -385,7 +392,7 @@
     return pl.pallas_call(
         functools.partial(inverse_kernel, h),
         grid=(6,),
-        in_specs=[whole(v.shape) for v in (r,) + ix + iy]
+        in_specs=[whole(v.shape) for v in (r, ix, iy)]
         + [plane(v.shape[2]) for v in extra],
         out_specs=plane(width),
         out_shape=jax.ShapeDtypeStruct((6, ny, width), F32),
@@ -396,7 +403,7 @@
             bytes_accessed=14 * 1024 * 1024,
             transcendentals=0,
         ),
-    )(r, *ix, *iy, *extra)
+    )(r, ix, iy, *extra)
 
 
 def shards(
@@ -412,8 +419,8 @@
     devices = lax.axis_size("gz")
     ny, nx = strain.shape[2], strain.shape[3]
     fx, fy, ix, iy = tables(nx, ny, devices)
-    fx, ix = [pair(v) for v in fx], [pair(v) for v in ix]
-    fy, iy = pair(fy), pair(iy)
+    fx, ix = [[triple(v, 0, (0, 1, 0)) for v in w] for w in (fx, ix)]
+    fy, iy = [triple(v, 2, (0, 1, 0)) for v in (fy, iy)]
     strain = strain.reshape(6, ny, nx)
     p, c = order_param[0], concentration[0]
     p_halo = neighbours(p)
@@ -430,19 +437,21 @@
         second_kernel, (), (p1, c_part, *c_halo, kinetic, decay), 3
     )
 
+    p1_halo, c1 = lax.optimization_barrier((p1_halo, c1))
+    c1_halo = neighbours(c1)
+
     def swap(chunk):
         return lax.all_to_all(chunk, "gz", split_axis=0, concat_axis=0, tiled=True)
 
     sent0, p2 = forward(0, strain, lt, m2, fx[0], fy, devices, (p2_part, kinetic, *p1_halo))
     (sent1,) = forward(1, strain, lt, m2, fx[1], fy, devices, (p2,))
     band0 = swap(sent0)
-    band0, c1 = lax.optimization_barrier((band0, c1))
-    c1_halo = neighbours(c1)
+    sent1, c1_halo = lax.optimization_barrier((sent1, c1_halo))
+    c2 = c2_part + time_step * (c1_halo[0] + c1_halo[1]) - p2
     band1 = swap(sent1)
-    back0 = swap(green(0, band0, ny))
-    done1, c1_halo = lax.optimization_barrier((green(1, band1, ny), c1_halo))
-    c2 = c2_part + time_step * (c1_halo[0] + c1_halo[1]) - p2
-    back1 = swap(done1)
+    done0, band1 = lax.optimization_barrier((green(0, band0, ny), band1))
+    back0 = swap(done0)
+    back1 = swap(green(1, band1, ny))
     z0 = inverse(0, back0, ix[0], iy, ny, nx)
     out = inverse(1, back1, ix[1], iy, ny, nx, (z0, strain))
     return (p2[None], c2[None], out[:, None])

time: 378 us -> 376 us (level)
  local copies, waits for them, and re-layouts: 13.3 us -> 4.74 us
  Pallas kernels: 77.1 us -> 81.7 us
    unnamed x60 -> x34, local copies, waits for them, and re-layouts: 13.2 us -> 4.67 us
    ppermute x4, waiting for transfers between devices: 44.9 us -> 37.6 us  [neighbours(): lax.ppermute(plane, 'gz', [((i + 1) % count, i) for i in range(count)])]
    all_to_all x4, waiting for transfers between devices: 152 us -> 157 us  [swap(): return lax.all_to_all(chunk, 'gz', split_axis=0, concat_axis=0, tiled=True)]
  transfers between devices with their start and end apart: 12 -> 12, of which waited for: 6 -> 6; matrix products, arithmetic and copies ran while one was open for 2% -> 1% of each run, Pallas kernels for 13% -> 14%
where the time goes in v3:
time: 376 us; the launch traced here: 375 us
  waiting for transfers between devices  200 us (53%)
  starting transfers between devices  82.1 us (22%)
  Pallas kernels  81.7 us (22%)
  other arithmetic  5.55 us (1%)
  local copies, waits for them, and re-layouts  4.74 us (1%)
    all_to_all x4, waiting for transfers between devices, swap(): return lax.all_to_all(chunk, 'gz', split_axis=0, concat_axis=0, tiled=True)  157 us
    all_to_all x4, starting transfers between devices, swap(): return lax.all_to_all(chunk, 'gz', split_axis=0, concat_axis=0, tiled=True)  42 us
    ppermute x4, waiting for transfers between devices, neighbours(): lax.ppermute(plane, 'gz', [((i + 1) % count, i) for i in range(count)])  37.6 us
    pallas_call x2, Pallas kernels, forward(): pl.pallas_call(functools.partial(forward_kernel, h), grid=(6,), in_specs=...  28.4 us
    pallas_call x2, Pallas kernels, inverse(): pl.pallas_call(functools.partial(inverse_kernel, h), grid=(6,), in_specs=...  24.4 us
    ppermute x4, starting transfers between devices, neighbours(): lax.ppermute(plane, 'gz', [((i + 1) % count, i) for i in range(count)])  22.4 us
    ppermute x4, starting transfers between devices, neighbours(): lax.ppermute(plane, 'gz', [(i, (i + 1) % count) for i in range(count)])  17.8 us
    pallas_call x2, Pallas kernels, planes_call(): pl.pallas_call(kernel, in_specs=[pl.BlockSpec(memory_space=pltpu.SMEM)] *...  16.7 us
  transfers between devices with their start and end apart: 12, of which 6 were waited for; matrix products, arithmetic and copies ran while one was open for 1% of the time, Pallas kernels for 14%

profile of v3, /device:TPU:0, one launch (start us, length us, event | category | flops | bytes accessed | tf_op | source)
XLA Modules:
  0.0 375.0 jit_solution(3231347816703160521)
XLA Ops:
  0.6 6.4 %collective-permute-start.1 = (f32[512,512]{1,0:T(8,128)}, f32[512,512]{1,0:T(8,128)S(1)}, u32[]{:S(2)}, u32[]{:S(2)}) collective-permute-start(f32[512,512]{1,0:T(8,128)} %bitcast.19), channel_id=1, source_target_pairs={{1,0},{2,1},{3,2},{4,3},{5,4},{6,5},{7,6},{8,7},{9,8},{10,9},{11,1... | collective-permute-start | bytes 3145736 | tf_op jit(solution)/shard_map/ppermute | solution.py:28
  7.1 0.0 collective-permute-start
  7.1 5.3 %collective-permute-start.3 = (f32[512,512]{1,0:T(8,128)}, f32[512,512]{1,0:T(8,128)S(1)}, u32[]{:S(2)}, u32[]{:S(2)}) collective-permute-start(f32[512,512]{1,0:T(8,128)} %bitcast.22), channel_id=1, source_target_pairs={{1,0},{2,1},{3,2},{4,3},{5,4},{6,5},{7,6},{8,7},{9,8},{10,9},{11,1... | collective-permute-start | bytes 3145736 | tf_op jit(solution)/shard_map/ppermute | solution.py:28
  12.4 0.0 collective-permute-start.2
  12.4 0.7 copy-done.7
  13.1 0.7 copy-done.8
  13.7 0.7 copy-done.9
  14.4 11.7 %shard_map.157 = (f32[512,512]{1,0:T(8,128)S(1)}, f32[512,512]{1,0:T(8,128)S(1)}, f32[512,512]{1,0:T(8,128)S(1)}, f32[512,512]{1,0:T(8,128)}, f32[512,512]{1,0:T(8,128)}, /*index=5*/f32[512,512]{1,0:T(8,128)}) custom-call(f32[2,16]{1,0:T(2,128)S(1)} %copy-done.7, f32[16]{0:T(128)S(1)} %copy-done.8, f32[8]{0:T(128)S(1)} %copy-done.9, f32[512,512]{1,0:T(8,128)} %bitcast.21, ...), custom_call_target="tpu_custom_call" | custom-call | flops 1677721600 | bytes 16777216 | tf_op jit(solution)/shard_map/pallas_call | solution.py:94
  26.1 0.0 collective-permute-done.1
  26.1 0.0 collective-permute-done
  26.1 2.1 multiply_add_fusion.p1_ref
  28.2 0.0 copy-start.12
  28.2 5.4 %collective-permute-start.5 = (f32[512,512]{1,0:T(8,128)S(1)}, f32[512,512]{1,0:T(8,128)S(1)}, u32[]{:S(2)}, u32[]{:S(2)}) collective-permute-start(f32[512,512]{1,0:T(8,128)S(1)} %multiply_add_fusion.p1_ref), channel_id=1, source_target_pairs={{1,0},{2,1},{3,2},{4,3},{5,4},{6,5},{7,6},{8,7},{9,8},{10,9},{11,1... | collective-permute-start | bytes 3145736 | tf_op jit(solution)/shard_map/ppermute | solution.py:28
  33.6 17.8 %collective-permute-start.4 = (f32[512,512]{1,0:T(8,128)S(1)}, f32[512,512]{1,0:T(8,128)S(1)}, u32[]{:S(2)}, u32[]{:S(2)}) collective-permute-start(f32[512,512]{1,0:T(8,128)S(1)} %multiply_add_fusion.p1_ref), channel_id=1, source_target_pairs={{0,1},{1,2},{2,3},{3,4},{4,5},{5,6},{6,7},{7,8},{8,9},{9,10},{10,1... | collective-permute-start | bytes 3145736 | tf_op jit(solution)/shard_map/ppermute | solution.py:27
  51.4 0.0 collective-permute-done.3.cu_ref
  51.4 0.0 collective-permute-done.2.cb_ref
  51.5 1.0 copy-done.15
  52.4 0.3 copy-done.16
  52.7 5.0 %shard_map.158 = (f32[512,512]{1,0:T(8,128)S(1)}, f32[512,512]{1,0:T(8,128)S(1)}, f32[512,512]{1,0:T(8,128)S(1)}) custom-call(f32[512,512]{1,0:T(8,128)} %copy-done.12, f32[512,512]{1,0:T(8,128)} %get-tuple-element.26.ca_ref, f32[512,512]{1,0:T(8,128)} %copy-done.16, f32[512,512]{1,0:T(8,128)} %copy-done.15, f32[512,512]{1,0:T(8,128)} %copy-done, ...), custom_call_target="tpu_custom_call" | custom-call | flops 943718400 | bytes 9437184 | tf_op jit(solution)/shard_map/pallas_call | solution.py:94
  57.8 0.0 collective-permute-done.5.rest_3_
  57.8 0.0 collective-permute-done.4.rest_2_
  57.8 0.0 copy-start.14
  57.8 1.0 copy-done.13
  58.8 0.4 copy-done.14
  59.2 15.1 %shard_map.159 = (f32[32,20,8,128]{3,2,1,0:T(8,128)}, f32[512,512]{1,0:T(8,128)}) custom-call(f32[6,512,512]{2,1,0:T(8,128)} %bitcast.13, f32[512,512]{1,0:T(8,128)S(1)} %get-tuple-element.22.lt_ref, f32[512,512]{1,0:T(8,128)S(1)} %get-tuple-element.23.m2_ref, bf16[768,256]{1,0:T(8,128)(2,1)S(1)} %copy-done.6, bf16[2,512,768]{2,1,0:T(8,128)(2,1)} %constant.31.clone.y_ref, ...), custom_call_target="tpu_custom_call" | custom-call | flops 3623878656 | bytes 14680064 | tf_op jit(solution)/shard_map/pallas_call | solution.py:224
  74.3 0.0 copy-start.1
  74.3 0.0 copy-start.4
  74.3 24.1 %all-to-all-start = ((f32[32,20,8,128]{3,2,1,0:T(8,128)}), f32[32,20,8,128]{3,2,1,0:T(8,128)}, u32[]{:S(2)}, u32[]{:S(2)}) async-start(f32[32,20,8,128]{3,2,1,0:T(8,128)} %get-tuple-element.37), calls=%async_computation | async-start | bytes 5242880 | tf_op jit(solution)/shard_map/all_to_all | solution.py:444
  98.4 5.2 %collective-permute-start.7 = (f32[512,512]{1,0:T(8,128)}, f32[512,512]{1,0:T(8,128)}, u32[]{:S(2)}, u32[]{:S(2)}) collective-permute-start(f32[512,512]{1,0:T(8,128)} %copy-done.10), channel_id=1, source_target_pairs={{1,0},{2,1},{3,2},{4,3},{5,4},{6,5},{7,6},{8,7},{9,8},{10,9},{11,1... | collective-permute-start | bytes 3145736 | tf_op jit(solution)/shard_map/ppermute | solution.py:28
  103.6 0.0 collective-permute-start.6
  103.6 13.3 %shard_map.160 = f32[32,20,8,128]{3,2,1,0:T(8,128)} custom-call(f32[6,512,512]{2,1,0:T(8,128)} %bitcast.14, f32[512,512]{1,0:T(8,128)S(1)} %get-tuple-element.22.lt_ref, f32[512,512]{1,0:T(8,128)S(1)} %get-tuple-element.23.m2_ref, bf16[768,256]{1,0:T(8,128)(2,1)S(1)} %copy-done.4, bf16[2,512,768]{2,1,0:T(8,128)(2,1)} %constant.31.clone.y_ref, ...), custom_call_target="tpu_custom_call" | custom-call | flops 3623878656 | bytes 14680064 | tf_op jit(solution)/shard_map/pallas_call | solution.py:224
  116.9 37.6 %collective-permute-done.7 = f32[512,512]{1,0:T(8,128)} collective-permute-done((f32[512,512]{1,0:T(8,128)}, f32[512,512]{1,0:T(8,128)}, u32[]{:S(2)}, u32[]{:S(2)}) %collective-permute-start.7) | collective-permute-done | bytes 1048608 | tf_op jit(solution)/shard_map/ppermute | solution.py:28
  154.5 5.1 %collective-permute-done.6 = f32[512,512]{1,0:T(8,128)} collective-permute-done((f32[512,512]{1,0:T(8,128)}, f32[512,512]{1,0:T(8,128)}, u32[]{:S(2)}, u32[]{:S(2)}) %collective-permute-start.6) | collective-permute-done | bytes 1048608 | tf_op jit(solution)/shard_map/ppermute | solution.py:27
  159.6 4.3 %all-to-all-done.x_ref = f32[32,20,8,128]{3,2,1,0:T(8,128)} async-done(((f32[32,20,8,128]{3,2,1,0:T(8,128)}), f32[32,20,8,128]{3,2,1,0:T(8,128)}, u32[]{:S(2)}, u32[]{:S(2)}) %all-to-all-start) | async-done | bytes 2621472 | tf_op jit(solution)/shard_map/all_to_all | solution.py:444
  163.8 9.5 %all-to-all-start.1 = ((f32[32,20,8,128]{3,2,1,0:T(8,128)}), f32[32,20,8,128]{3,2,1,0:T(8,128)}, u32[]{:S(2)}, u32[]{:S(2)}) async-start(f32[32,20,8,128]{3,2,1,0:T(8,128)} %shard_map.160), calls=%async_computation.1 | async-start | bytes 5242880 | tf_op jit(solution)/shard_map/all_to_all | solution.py:444
  173.4 0.1 broadcast_in_dim.10.my_ref
  173.4 6.1 %shard_map.161 = f32[32,20,8,128]{3,2,1,0:T(8,128)} custom-call(f32[32,20,8,128]{3,2,1,0:T(8,128)} %all-to-all-done.x_ref, f32[2,8,128]{2,1,0:T(8,128)S(1)} %broadcast_in_dim.10.my_ref), custom_call_target="tpu_custom_call" | custom-call | flops 41943040 | bytes 5242880 | tf_op jit(solution)/shard_map/pallas_call | solution.py:321
  179.5 54.0 %all-to-all-done.1.x_ref = f32[32,20,8,128]{3,2,1,0:T(8,128)} async-done(((f32[32,20,8,128]{3,2,1,0:T(8,128)}), f32[32,20,8,128]{3,2,1,0:T(8,128)}, u32[]{:S(2)}, u32[]{:S(2)}) %all-to-all-start.1) | async-done | bytes 2621472 | tf_op jit(solution)/shard_map/all_to_all | solution.py:444
  233.5 4.1 %all-to-all-start.3 = ((f32[32,20,8,128]{3,2,1,0:T(8,128)}), f32[32,20,8,128]{3,2,1,0:T(8,128)}, u32[]{:S(2)}, u32[]{:S(2)}) async-start(f32[32,20,8,128]{3,2,1,0:T(8,128)} %shard_map.161), calls=%async_computation.3 | async-start | bytes 5242880 | tf_op jit(solution)/shard_map/all_to_all | solution.py:444
  237.6 6.0 %shard_map.162 = f32[32,20,8,128]{3,2,1,0:T(8,128)} custom-call(f32[32,20,8,128]{3,2,1,0:T(8,128)} %all-to-all-done.1.x_ref, f32[2,8,128]{2,1,0:T(8,128)S(1)} %broadcast_in_dim.10.my_ref), custom_call_target="tpu_custom_call" | custom-call | flops 41943040 | bytes 5242880 | tf_op jit(solution)/shard_map/pallas_call | solution.py:321
  243.6 54.1 %all-to-all-done.3.r_ref = f32[32,20,8,128]{3,2,1,0:T(8,128)} async-done(((f32[32,20,8,128]{3,2,1,0:T(8,128)}), f32[32,20,8,128]{3,2,1,0:T(8,128)}, u32[]{:S(2)}, u32[]{:S(2)}) %all-to-all-start.3) | async-done | bytes 2621472 | tf_op jit(solution)/shard_map/all_to_all | solution.py:444
  297.7 4.3 %all-to-all-start.2 = ((f32[32,20,8,128]{3,2,1,0:T(8,128)}), f32[32,20,8,128]{3,2,1,0:T(8,128)}, u32[]{:S(2)}, u32[]{:S(2)}) async-start(f32[32,20,8,128]{3,2,1,0:T(8,128)} %shard_map.162), calls=%async_computation.2 | async-start | bytes 5242880 | tf_op jit(solution)/shard_map/all_to_all | solution.py:444
  302.1 0.0 copy-start.2
  302.1 0.0 copy-start.11
  302.1 3.5 subtract_bitcast_fusion
  305.5 11.6 %shard_map.163.rest_0_ = f32[6,512,256]{2,1,0:T(8,128)} custom-call(f32[32,20,8,128]{3,2,1,0:T(8,128)} %all-to-all-done.3.r_ref, bf16[768,256]{1,0:T(8,128)(2,1)S(1)} %copy-done.11, bf16[2,512,768]{2,1,0:T(8,128)(2,1)S(1)} %copy-done.2), custom_call_target="tpu_custom_call" | custom-call | flops 3623878656 | bytes 14680064 | tf_op jit(solution)/shard_map/pallas_call | solution.py:392
  317.1 45.0 %all-to-all-done.2.r_ref = f32[32,20,8,128]{3,2,1,0:T(8,128)} async-done(((f32[32,20,8,128]{3,2,1,0:T(8,128)}), f32[32,20,8,128]{3,2,1,0:T(8,128)}, u32[]{:S(2)}, u32[]{:S(2)}) %all-to-all-start.2) | async-done | bytes 2621472 | tf_op jit(solution)/shard_map/all_to_all | solution.py:444
  362.1 12.9 %shard_map.164 = f32[6,512,512]{2,1,0:T(8,128)} custom-call(f32[32,20,8,128]{3,2,1,0:T(8,128)} %all-to-all-done.2.r_ref, bf16[768,256]{1,0:T(8,128)(2,1)S(1)} %copy-done.5, bf16[2,512,768]{2,1,0:T(8,128)(2,1)S(1)} %copy-done.2, f32[6,512,256]{2,1,0:T(8,128)} %shard_map.163.rest_0_, f32[6,512,512]{2,1,0:T(8,128)} %bitcast.15), custom_call_target="tpu_custom_call" | custom-call | flops 3623878656 | bytes 14680064 | tf_op jit(solution)/shard_map/pallas_call | solution.py:392
  (23 shorter events, 0.1 us)
Async XLA Ops:
  0.6 25.5 %collective-permute-start.1 = (f32[512,512]{1,0:T(8,128)}, f32[512,512]{1,0:T(8,128)S(1)}, u32[]{:S(2)}, u32[]{:S(2)}) collective-permute-start(f32[512,512]{1,0:T(8,128)} %bitcast.19), channel_id=1, source_target_pairs={{1,0},{2,1},{3,2},{4,3},{5,4},{6,5},{7,6},{8,7},{9,8},{10,9},{11,1... | collective-permute-start | bytes 3145736 | tf_op jit(solution)/shard_map/ppermute | solution.py:28
  7.1 19.0 %collective-permute-start = (f32[512,512]{1,0:T(8,128)}, f32[512,512]{1,0:T(8,128)S(1)}, u32[]{:S(2)}, u32[]{:S(2)}) collective-permute-start(f32[512,512]{1,0:T(8,128)} %bitcast.20), channel_id=1, source_target_pairs={{0,1},{1,2},{2,3},{3,4},{4,5},{5,6},{6,7},{7,8},{8,9},{9,10},{10,1... | collective-permute-start | bytes 3145736 | tf_op jit(solution)/shard_map/ppermute | solution.py:27
  7.1 44.4 %collective-permute-start.3 = (f32[512,512]{1,0:T(8,128)}, f32[512,512]{1,0:T(8,128)S(1)}, u32[]{:S(2)}, u32[]{:S(2)}) collective-permute-start(f32[512,512]{1,0:T(8,128)} %bitcast.22), channel_id=1, source_target_pairs={{1,0},{2,1},{3,2},{4,3},{5,4},{6,5},{7,6},{8,7},{9,8},{10,9},{11,1... | collective-permute-start | bytes 3145736 | tf_op jit(solution)/shard_map/ppermute | solution.py:28
  12.4 39.0 %collective-permute-start.2 = (f32[512,512]{1,0:T(8,128)}, f32[512,512]{1,0:T(8,128)S(1)}, u32[]{:S(2)}, u32[]{:S(2)}) collective-permute-start(f32[512,512]{1,0:T(8,128)} %bitcast.23), channel_id=1, source_target_pairs={{0,1},{1,2},{2,3},{3,4},{4,5},{5,6},{6,7},{7,8},{8,9},{9,10},{10,1... | collective-permute-start | bytes 3145736 | tf_op jit(solution)/shard_map/ppermute | solution.py:27
  12.4 0.7 copy-start.7
  13.1 0.7 copy-start.8
  13.7 0.7 copy-start.9
  26.1 2.1 copy-start
  28.2 23.2 %copy-start.12 = (f32[512,512]{1,0:T(8,128)}, f32[512,512]{1,0:T(8,128)S(1)}, u32[]{:S(2)}) copy-start(f32[512,512]{1,0:T(8,128)S(1)} %multiply_add_fusion.p1_ref) | copy-start | bytes 3145732
  28.2 29.5 %collective-permute-start.5 = (f32[512,512]{1,0:T(8,128)S(1)}, f32[512,512]{1,0:T(8,128)S(1)}, u32[]{:S(2)}, u32[]{:S(2)}) collective-permute-start(f32[512,512]{1,0:T(8,128)S(1)} %multiply_add_fusion.p1_ref), channel_id=1, source_target_pairs={{1,0},{2,1},{3,2},{4,3},{5,4},{6,5},{7,6},{8,7},{9,8},{10,9},{11,1... | collective-permute-start | bytes 3145736 | tf_op jit(solution)/shard_map/ppermute | solution.py:28
  33.6 24.2 %collective-permute-start.4 = (f32[512,512]{1,0:T(8,128)S(1)}, f32[512,512]{1,0:T(8,128)S(1)}, u32[]{:S(2)}, u32[]{:S(2)}) collective-permute-start(f32[512,512]{1,0:T(8,128)S(1)} %multiply_add_fusion.p1_ref), channel_id=1, source_target_pairs={{0,1},{1,2},{2,3},{3,4},{4,5},{5,6},{6,7},{7,8},{8,9},{9,10},{10,1... | collective-permute-start | bytes 3145736 | tf_op jit(solution)/shard_map/ppermute | solution.py:27
  51.4 1.0 copy-start.15
  51.4 1.3 copy-start.16
  52.7 6.4 %copy-start.6 = (bf16[768,256]{1,0:T(8,128)(2,1)S(1)}, bf16[768,256]{1,0:T(8,128)(2,1)}, u32[]{:S(2)}) copy-start(bf16[768,256]{1,0:T(8,128)(2,1)} %constant.27.clone.x_ref) | copy-start | bytes 1179652
  57.7 16.5 %copy-start.3 = (f32[512,512]{1,0:T(8,128)}, f32[512,512]{1,0:T(8,128)S(1)}, u32[]{:S(2)}) copy-start(f32[512,512]{1,0:T(8,128)S(1)} %get-tuple-element.33) | copy-start | bytes 3145732
  57.8 16.5 %copy-start.10 = (f32[512,512]{1,0:T(8,128)}, f32[512,512]{1,0:T(8,128)S(1)}, u32[]{:S(2)}) copy-start(f32[512,512]{1,0:T(8,128)S(1)} %get-tuple-element.34) | copy-start | bytes 3145732
  57.8 1.0 copy-start.13
  57.8 1.4 copy-start.14
  74.3 29.3 %copy-start.1 = (f32[512,512]{1,0:T(8,128)S(1)}, f32[512,512]{1,0:T(8,128)}, u32[]{:S(2)}) copy-start(f32[512,512]{1,0:T(8,128)} %get-tuple-element.32.rest_0_) | copy-start | bytes 3145732
  74.3 29.3 %copy-start.4 = (bf16[768,256]{1,0:T(8,128)(2,1)S(1)}, bf16[768,256]{1,0:T(8,128)(2,1)}, u32[]{:S(2)}) copy-start(bf16[768,256]{1,0:T(8,128)(2,1)} %constant.28.clone.x_ref) | copy-start | bytes 1179652
  74.3 89.5 %all-to-all-start = ((f32[32,20,8,128]{3,2,1,0:T(8,128)}), f32[32,20,8,128]{3,2,1,0:T(8,128)}, u32[]{:S(2)}, u32[]{:S(2)}) async-start(f32[32,20,8,128]{3,2,1,0:T(8,128)} %get-tuple-element.37), calls=%async_computation | async-start | bytes 5242880 | tf_op jit(solution)/shard_map/all_to_all | solution.py:444
  98.4 56.1 %collective-permute-start.7 = (f32[512,512]{1,0:T(8,128)}, f32[512,512]{1,0:T(8,128)}, u32[]{:S(2)}, u32[]{:S(2)}) collective-permute-start(f32[512,512]{1,0:T(8,128)} %copy-done.10), channel_id=1, source_target_pairs={{1,0},{2,1},{3,2},{4,3},{5,4},{6,5},{7,6},{8,7},{9,8},{10,9},{11,1... | collective-permute-start | bytes 3145736 | tf_op jit(solution)/shard_map/ppermute | solution.py:28
  103.6 56.0 %collective-permute-start.6 = (f32[512,512]{1,0:T(8,128)}, f32[512,512]{1,0:T(8,128)}, u32[]{:S(2)}, u32[]{:S(2)}) collective-permute-start(f32[512,512]{1,0:T(8,128)} %copy-done.10), channel_id=1, source_target_pairs={{0,1},{1,2},{2,3},{3,4},{4,5},{5,6},{6,7},{7,8},{8,9},{9,10},{10,1... | collective-permute-start | bytes 3145736 | tf_op jit(solution)/shard_map/ppermute | solution.py:27
  163.8 69.6 %all-to-all-start.1 = ((f32[32,20,8,128]{3,2,1,0:T(8,128)}), f32[32,20,8,128]{3,2,1,0:T(8,128)}, u32[]{:S(2)}, u32[]{:S(2)}) async-start(f32[32,20,8,128]{3,2,1,0:T(8,128)} %shard_map.160), calls=%async_computation.1 | async-start | bytes 5242880 | tf_op jit(solution)/shard_map/all_to_all | solution.py:444
  233.5 64.3 %all-to-all-start.3 = ((f32[32,20,8,128]{3,2,1,0:T(8,128)}), f32[32,20,8,128]{3,2,1,0:T(8,128)}, u32[]{:S(2)}, u32[]{:S(2)}) async-start(f32[32,20,8,128]{3,2,1,0:T(8,128)} %shard_map.161), calls=%async_computation.3 | async-start | bytes 5242880 | tf_op jit(solution)/shard_map/all_to_all | solution.py:444
  297.7 64.4 %all-to-all-start.2 = ((f32[32,20,8,128]{3,2,1,0:T(8,128)}), f32[32,20,8,128]{3,2,1,0:T(8,128)}, u32[]{:S(2)}, u32[]{:S(2)}) async-start(f32[32,20,8,128]{3,2,1,0:T(8,128)} %shard_map.162), calls=%async_computation.2 | async-start | bytes 5242880 | tf_op jit(solution)/shard_map/all_to_all | solution.py:444
  302.1 3.5 copy-start.2
  302.1 3.5 copy-start.11
  305.5 56.6 %copy-start.5 = (bf16[768,256]{1,0:T(8,128)(2,1)S(1)}, bf16[768,256]{1,0:T(8,128)(2,1)}, u32[]{:S(2)}) copy-start(bf16[768,256]{1,0:T(8,128)(2,1)} %constant.30.clone.x_ref) | copy-start | bytes 1179652

commit v4 on v3

--- a/solution.py
+++ b/solution.py
@@ -102,7 +102,7 @@
     )(*scalars, *arrays)
 
 
-def triple(table, axis, order):
+def parts(table, axis, order):
     table = np.asarray(table, np.float32)
     hi = table.astype(ml_dtypes.bfloat16)
     lo = (table - hi.astype(np.float32)).astype(ml_dtypes.bfloat16)
@@ -132,16 +132,20 @@
     return hi, (x - hi.astype(F32)).astype(BF16)
 
 
+def dot(u, v):
+    return jnp.dot(u, v, preferred_element_type=F32)
+
+
 def dot_right(a, table):
     hi, lo = split(a)
-    left = jnp.concatenate([hi, hi, lo], axis=1)
-    return jnp.dot(left, table, preferred_element_type=F32)
+    n = table.shape[0] // 2
+    return dot(hi, table[:n]) + (dot(hi, table[n:]) + dot(lo, table[:n]))
 
 
 def dot_left(table, b):
     hi, lo = split(b)
-    right = jnp.concatenate([hi, hi, lo], axis=0)
-    return jnp.dot(table, right, preferred_element_type=F32)
+    n = table.shape[1] // 2
+    return dot(table[:, :n], hi) + (dot(table[:, n:], hi) + dot(table[:, :n], lo))
 
 
 def waves(par, ny, lanes):
@@ -419,8 +423,8 @@
     devices = lax.axis_size("gz")
     ny, nx = strain.shape[2], strain.shape[3]
     fx, fy, ix, iy = tables(nx, ny, devices)
-    fx, ix = [[triple(v, 0, (0, 1, 0)) for v in w] for w in (fx, ix)]
-    fy, iy = [triple(v, 2, (0, 1, 0)) for v in (fy, iy)]
+    fx, ix = [[parts(v, 0, (0, 1)) for v in w] for w in (fx, ix)]
+    fy, iy = [parts(v, 2, (0, 1)) for v in (fy, iy)]
     strain = strain.reshape(6, ny, nx)
     p, c = order_param[0], concentration[0]
     p_halo = neighbours(p)
@@ -445,8 +449,8 @@
 
     sent0, p2 = forward(0, strain, lt, m2, fx[0], fy, devices, (p2_part, kinetic, *p1_halo))
     (sent1,) = forward(1, strain, lt, m2, fx[1], fy, devices, (p2,))
+    sent0, c1_halo = lax.optimization_barrier((sent0, c1_halo))
     band0 = swap(sent0)
-    sent1, c1_halo = lax.optimization_barrier((sent1, c1_halo))
     c2 = c2_part + time_step * (c1_halo[0] + c1_halo[1]) - p2
     band1 = swap(sent1)
     done0, band1 = lax.optimization_barrier((green(0, band0, ny), band1))

time: 376 us -> 385 us (1.024)
  local copies, waits for them, and re-layouts: 4.74 us -> 13 us
  Pallas kernels: 81.7 us -> 77.3 us
    all_to_all x4, waiting for transfers between devices: 157 us -> 202 us  [swap(): return lax.all_to_all(chunk, 'gz', split_axis=0, concat_axis=0, tiled=True)]
    ppermute x4, waiting for transfers between devices: 37.6 us -> 0.01 us  [neighbours(): lax.ppermute(plane, 'gz', [((i + 1) % count, i) for i in range(count)])]
    ppermute x4, starting transfers between devices: 17.8 us -> 41 us  [neighbours(): lax.ppermute(plane, 'gz', [(i, (i + 1) % count) for i in range(count)])]
    all_to_all x4, starting transfers between devices: 42 us -> 27.3 us  [swap(): return lax.all_to_all(chunk, 'gz', split_axis=0, concat_axis=0, tiled=True)]
    unnamed x34 -> x48, local copies, waits for them, and re-layouts: 4.67 us -> 12.9 us
    ppermute x4, starting transfers between devices: 22.4 us -> 17.2 us  [neighbours(): lax.ppermute(plane, 'gz', [((i + 1) % count, i) for i in range(count)])]
    ppermute x4, waiting for transfers between devices: 5.08 us -> 0.01 us  [neighbours(): lax.ppermute(plane, 'gz', [(i, (i + 1) % count) for i in range(count)])]
  transfers between devices with their start and end apart: 12 -> 12, of which waited for: 6 -> 4; matrix products, arithmetic and copies ran while one was open for 1% -> 2% of each run, Pallas kernels for 14% -> 17%
where the time goes in v4:
time: 385 us; the launch traced here: 384 us
  waiting for transfers between devices  202 us (52%)
  starting transfers between devices  85.5 us (22%)
  Pallas kernels  77.3 us (20%)
  local copies, waits for them, and re-layouts  13 us (3%)
  other arithmetic  5.91 us (2%)
    all_to_all x4, waiting for transfers between devices, swap(): return lax.all_to_all(chunk, 'gz', split_axis=0, concat_axis=0, tiled=True)  202 us
    ppermute x4, starting transfers between devices, neighbours(): lax.ppermute(plane, 'gz', [(i, (i + 1) % count) for i in range(count)])  41 us
    pallas_call x2, Pallas kernels, forward(): pl.pallas_call(functools.partial(forward_kernel, h), grid=(6,), in_specs=...  28.1 us
    all_to_all x4, starting transfers between devices, swap(): return lax.all_to_all(chunk, 'gz', split_axis=0, concat_axis=0, tiled=True)  27.3 us
    pallas_call x2, Pallas kernels, inverse(): pl.pallas_call(functools.partial(inverse_kernel, h), grid=(6,), in_specs=...  21.9 us
    ppermute x4, starting transfers between devices, neighbours(): lax.ppermute(plane, 'gz', [((i + 1) % count, i) for i in range(count)])  17.2 us
    pallas_call x2, Pallas kernels, planes_call(): pl.pallas_call(kernel, in_specs=[pl.BlockSpec(memory_space=pltpu.SMEM)] *...  16.8 us
    unnamed x48, local copies, waits for them, and re-layouts  12.9 us
  transfers between devices with their start and end apart: 12, of which 4 were waited for; matrix products, arithmetic and copies ran while one was open for 2% of the time, Pallas kernels for 17%

profile of v4, /device:TPU:0, one launch (start us, length us, event | category | flops | bytes accessed | tf_op | source)
XLA Modules:
  0.0 384.1 jit_solution(17701508411245662983)
XLA Ops:
  0.6 6.4 %collective-permute-start.1 = (f32[512,512]{1,0:T(8,128)}, f32[512,512]{1,0:T(8,128)S(1)}, u32[]{:S(2)}, u32[]{:S(2)}) collective-permute-start(f32[512,512]{1,0:T(8,128)} %bitcast.19), channel_id=1, source_target_pairs={{1,0},{2,1},{3,2},{4,3},{5,4},{6,5},{7,6},{8,7},{9,8},{10,9},{11,1... | collective-permute-start | bytes 3145736 | tf_op jit(solution)/shard_map/ppermute | solution.py:28
  7.1 5.3 %collective-permute-start.3 = (f32[512,512]{1,0:T(8,128)}, f32[512,512]{1,0:T(8,128)S(1)}, u32[]{:S(2)}, u32[]{:S(2)}) collective-permute-start(f32[512,512]{1,0:T(8,128)} %bitcast.22), channel_id=1, source_target_pairs={{1,0},{2,1},{3,2},{4,3},{5,4},{6,5},{7,6},{8,7},{9,8},{10,9},{11,1... | collective-permute-start | bytes 3145736 | tf_op jit(solution)/shard_map/ppermute | solution.py:28
  12.4 0.0 collective-permute-start.2
  12.4 0.7 copy-done.11
  13.1 0.7 copy-done.12
  13.7 0.7 copy-done.13
  14.4 11.7 %shard_map.157 = (f32[512,512]{1,0:T(8,128)S(1)}, f32[512,512]{1,0:T(8,128)S(1)}, f32[512,512]{1,0:T(8,128)S(1)}, f32[512,512]{1,0:T(8,128)}, f32[512,512]{1,0:T(8,128)}, /*index=5*/f32[512,512]{1,0:T(8,128)}) custom-call(f32[2,16]{1,0:T(2,128)S(1)} %copy-done.11, f32[16]{0:T(128)S(1)} %copy-done.12, f32[8]{0:T(128)S(1)} %copy-done.13, f32[512,512]{1,0:T(8,128)} %bitcast.21, ...), custom_call_target="tpu_custom_call" | custom-call | flops 1677721600 | bytes 16777216 | tf_op jit(solution)/shard_map/pallas_call | solution.py:94
  26.1 0.0 collective-permute-done.1
  26.1 2.1 multiply_add_fusion.p1_ref
  28.2 0.0 copy-start.17
  28.3 5.4 %collective-permute-start.5 = (f32[512,512]{1,0:T(8,128)S(1)}, f32[512,512]{1,0:T(8,128)S(1)}, u32[]{:S(2)}, u32[]{:S(2)}) collective-permute-start(f32[512,512]{1,0:T(8,128)S(1)} %multiply_add_fusion.p1_ref), channel_id=1, source_target_pairs={{1,0},{2,1},{3,2},{4,3},{5,4},{6,5},{7,6},{8,7},{9,8},{10,9},{11,1... | collective-permute-start | bytes 3145736 | tf_op jit(solution)/shard_map/ppermute | solution.py:28
  33.6 17.8 %collective-permute-start.4 = (f32[512,512]{1,0:T(8,128)S(1)}, f32[512,512]{1,0:T(8,128)S(1)}, u32[]{:S(2)}, u32[]{:S(2)}) collective-permute-start(f32[512,512]{1,0:T(8,128)S(1)} %multiply_add_fusion.p1_ref), channel_id=1, source_target_pairs={{0,1},{1,2},{2,3},{3,4},{4,5},{5,6},{6,7},{7,8},{8,9},{9,10},{10,1... | collective-permute-start | bytes 3145736 | tf_op jit(solution)/shard_map/ppermute | solution.py:27
  51.4 0.0 collective-permute-done.3.cu_ref
  51.4 0.0 collective-permute-done.2.cb_ref
  51.5 1.0 copy-done.20
  52.4 0.3 copy-done.21
  52.7 5.1 %shard_map.158 = (f32[512,512]{1,0:T(8,128)S(1)}, f32[512,512]{1,0:T(8,128)S(1)}, f32[512,512]{1,0:T(8,128)S(1)}) custom-call(f32[512,512]{1,0:T(8,128)} %copy-done.17, f32[512,512]{1,0:T(8,128)} %get-tuple-element.26.ca_ref, f32[512,512]{1,0:T(8,128)} %copy-done.21, f32[512,512]{1,0:T(8,128)} %copy-done.20, f32[512,512]{1,0:T(8,128)} %copy-done.1, ...), custom_call_target="tpu_custom_call" | custom-call | flops 943718400 | bytes 9437184 | tf_op jit(solution)/shard_map/pallas_call | solution.py:94
  57.8 1.1 copy-done.6
  58.9 1.0 copy-done.8
  59.8 0.0 collective-permute-done.5.rest_3_
  59.8 0.1 collective-permute-start.7
  59.9 23.3 %collective-permute-start.6 = (f32[512,512]{1,0:T(8,128)S(1)}, f32[512,512]{1,0:T(8,128)S(1)}, u32[]{:S(2)}, u32[]{:S(2)}) collective-permute-start(f32[512,512]{1,0:T(8,128)S(1)} %get-tuple-element.35), channel_id=1, source_target_pairs={{0,1},{1,2},{2,3},{3,4},{4,5},{5,6},{6,7},{7,8},{8,9},{9,10},{10,1... | collective-permute-start | bytes 3145736 | tf_op jit(solution)/shard_map/ppermute | solution.py:27
  83.2 15.0 %shard_map.159 = (f32[32,20,8,128]{3,2,1,0:T(8,128)}, f32[512,512]{1,0:T(8,128)}) custom-call(f32[6,512,512]{2,1,0:T(8,128)} %bitcast.12, f32[512,512]{1,0:T(8,128)S(1)} %get-tuple-element.22.lt_ref, f32[512,512]{1,0:T(8,128)S(1)} %get-tuple-element.23.m2_ref, bf16[512,256]{1,0:T(8,128)(2,1)S(1)} %copy-done.10, bf16[2,512,512]{2,1,0:T(8,128)(2,1)S(1)} %copy-done.7, ...), custom_call_target="tpu_custom_call" | custom-call | flops 3623878656 | bytes 14680064 | tf_op jit(solution)/shard_map/pallas_call | solution.py:228
  98.2 0.9 copy-done.18
  99.1 1.0 copy-done.19
  100.1 15.1 %all-to-all-start = ((f32[32,20,8,128]{3,2,1,0:T(8,128)}), f32[32,20,8,128]{3,2,1,0:T(8,128)}, u32[]{:S(2)}, u32[]{:S(2)}) async-start(f32[32,20,8,128]{3,2,1,0:T(8,128)} %get-tuple-element.38), calls=%async_computation | async-start | bytes 5242880 | tf_op jit(solution)/shard_map/all_to_all | solution.py:448
  115.2 13.1 %shard_map.161 = f32[32,20,8,128]{3,2,1,0:T(8,128)} custom-call(f32[6,512,512]{2,1,0:T(8,128)} %bitcast.13, f32[512,512]{1,0:T(8,128)S(1)} %get-tuple-element.22.lt_ref, f32[512,512]{1,0:T(8,128)S(1)} %get-tuple-element.23.m2_ref, bf16[512,256]{1,0:T(8,128)(2,1)S(1)} %copy-done.15, bf16[2,512,512]{2,1,0:T(8,128)(2,1)S(1)} %copy-done.7, ...), custom_call_target="tpu_custom_call" | custom-call | flops 3623878656 | bytes 14680064 | tf_op jit(solution)/shard_map/pallas_call | solution.py:228
  128.3 47.0 %all-to-all-done.x_ref = f32[32,20,8,128]{3,2,1,0:T(8,128)} async-done(((f32[32,20,8,128]{3,2,1,0:T(8,128)}), f32[32,20,8,128]{3,2,1,0:T(8,128)}, u32[]{:S(2)}, u32[]{:S(2)}) %all-to-all-start) | async-done | bytes 2621472 | tf_op jit(solution)/shard_map/all_to_all | solution.py:448
  175.3 4.0 %all-to-all-start.1 = ((f32[32,20,8,128]{3,2,1,0:T(8,128)}), f32[32,20,8,128]{3,2,1,0:T(8,128)S(1)}, u32[]{:S(2)}, u32[]{:S(2)}) async-start(f32[32,20,8,128]{3,2,1,0:T(8,128)} %shard_map.161), calls=%async_computation.1 | async-start | bytes 5242880 | tf_op jit(solution)/shard_map/all_to_all | solution.py:448
  179.3 0.1 broadcast_in_dim.10.my_ref
  179.4 6.0 %shard_map.160 = f32[32,20,8,128]{3,2,1,0:T(8,128)} custom-call(f32[32,20,8,128]{3,2,1,0:T(8,128)} %all-to-all-done.x_ref, f32[2,8,128]{2,1,0:T(8,128)S(1)} %broadcast_in_dim.10.my_ref), custom_call_target="tpu_custom_call" | custom-call | flops 41943040 | bytes 5242880 | tf_op jit(solution)/shard_map/pallas_call | solution.py:325
  185.5 54.0 %all-to-all-done.1.x_ref = f32[32,20,8,128]{3,2,1,0:T(8,128)S(1)} async-done(((f32[32,20,8,128]{3,2,1,0:T(8,128)}), f32[32,20,8,128]{3,2,1,0:T(8,128)S(1)}, u32[]{:S(2)}, u32[]{:S(2)}) %all-to-all-start.1) | async-done | bytes 2621472 | tf_op jit(solution)/shard_map/all_to_all | solution.py:448
  239.5 1.5 copy-done.16
  241.0 4.0 %all-to-all-start.3 = ((f32[32,20,8,128]{3,2,1,0:T(8,128)}), f32[32,20,8,128]{3,2,1,0:T(8,128)S(1)}, u32[]{:S(2)}, u32[]{:S(2)}) async-start(f32[32,20,8,128]{3,2,1,0:T(8,128)} %shard_map.160), calls=%async_computation.3 | async-start | bytes 5242880 | tf_op jit(solution)/shard_map/all_to_all | solution.py:448
  245.0 4.5 %shard_map.162 = f32[32,20,8,128]{3,2,1,0:T(8,128)S(1)} custom-call(f32[32,20,8,128]{3,2,1,0:T(8,128)} %copy-done.16, f32[2,8,128]{2,1,0:T(8,128)S(1)} %broadcast_in_dim.10.my_ref), custom_call_target="tpu_custom_call" | custom-call | flops 41943040 | bytes 5242880 | tf_op jit(solution)/shard_map/pallas_call | solution.py:325
  249.5 0.0 copy-start
  249.5 1.5 copy-done
  251.0 54.1 %all-to-all-done.3.r_ref = f32[32,20,8,128]{3,2,1,0:T(8,128)S(1)} async-done(((f32[32,20,8,128]{3,2,1,0:T(8,128)}), f32[32,20,8,128]{3,2,1,0:T(8,128)S(1)}, u32[]{:S(2)}, u32[]{:S(2)}) %all-to-all-start.3) | async-done | bytes 2621472 | tf_op jit(solution)/shard_map/all_to_all | solution.py:448
  305.1 1.5 copy-done.2
  306.6 4.2 %all-to-all-start.2 = ((f32[32,20,8,128]{3,2,1,0:T(8,128)}), f32[32,20,8,128]{3,2,1,0:T(8,128)S(1)}, u32[]{:S(2)}, u32[]{:S(2)}) async-start(f32[32,20,8,128]{3,2,1,0:T(8,128)} %copy-done), calls=%async_computation.2 | async-start | bytes 5242880 | tf_op jit(solution)/shard_map/all_to_all | solution.py:448
  310.8 0.0 copy-start.4
  310.8 0.0 copy-start.14
  310.8 3.8 subtract_bitcast_fusion
  314.6 0.0 copy-start.9
  314.7 9.8 %shard_map.163.rest_0_ = f32[6,512,256]{2,1,0:T(8,128)} custom-call(f32[32,20,8,128]{3,2,1,0:T(8,128)S(1)} %copy-done.3, bf16[512,256]{1,0:T(8,128)(2,1)S(1)} %copy-done.14, bf16[2,512,512]{2,1,0:T(8,128)(2,1)S(1)} %copy-done.4), custom_call_target="tpu_custom_call" | custom-call | flops 3623878656 | bytes 14680064 | tf_op jit(solution)/shard_map/pallas_call | solution.py:396
  324.5 46.4 %all-to-all-done.2.r_ref = f32[32,20,8,128]{3,2,1,0:T(8,128)S(1)} async-done(((f32[32,20,8,128]{3,2,1,0:T(8,128)}), f32[32,20,8,128]{3,2,1,0:T(8,128)S(1)}, u32[]{:S(2)}, u32[]{:S(2)}) %all-to-all-start.2) | async-done | bytes 2621472 | tf_op jit(solution)/shard_map/all_to_all | solution.py:448
  370.9 1.2 copy-done.5
  372.1 12.0 %shard_map.164 = f32[6,512,512]{2,1,0:T(8,128)} custom-call(f32[32,20,8,128]{3,2,1,0:T(8,128)S(1)} %all-to-all-done.2.r_ref, bf16[512,256]{1,0:T(8,128)(2,1)S(1)} %copy-done.9, bf16[2,512,512]{2,1,0:T(8,128)(2,1)S(1)} %copy-done.5, f32[6,512,256]{2,1,0:T(8,128)} %shard_map.163.rest_0_, f32[6,512,512]{2,1,0:T(8,128)} %bitcast.14), custom_call_target="tpu_custom_call" | custom-call | flops 3623878656 | bytes 14680064 | tf_op jit(solution)/shard_map/pallas_call | solution.py:396
  (37 shorter events, 0.1 us)
Async XLA Ops:
  0.6 25.5 %collective-permute-start.1 = (f32[512,512]{1,0:T(8,128)}, f32[512,512]{1,0:T(8,128)S(1)}, u32[]{:S(2)}, u32[]{:S(2)}) collective-permute-start(f32[512,512]{1,0:T(8,128)} %bitcast.19), channel_id=1, source_target_pairs={{1,0},{2,1},{3,2},{4,3},{5,4},{6,5},{7,6},{8,7},{9,8},{10,9},{11,1... | collective-permute-start | bytes 3145736 | tf_op jit(solution)/shard_map/ppermute | solution.py:28
  7.1 19.1 %collective-permute-start = (f32[512,512]{1,0:T(8,128)}, f32[512,512]{1,0:T(8,128)S(1)}, u32[]{:S(2)}, u32[]{:S(2)}) collective-permute-start(f32[512,512]{1,0:T(8,128)} %bitcast.20), channel_id=1, source_target_pairs={{0,1},{1,2},{2,3},{3,4},{4,5},{5,6},{6,7},{7,8},{8,9},{9,10},{10,1... | collective-permute-start | bytes 3145736 | tf_op jit(solution)/shard_map/ppermute | solution.py:27
  7.1 44.4 %collective-permute-start.3 = (f32[512,512]{1,0:T(8,128)}, f32[512,512]{1,0:T(8,128)S(1)}, u32[]{:S(2)}, u32[]{:S(2)}) collective-permute-start(f32[512,512]{1,0:T(8,128)} %bitcast.22), channel_id=1, source_target_pairs={{1,0},{2,1},{3,2},{4,3},{5,4},{6,5},{7,6},{8,7},{9,8},{10,9},{11,1... | collective-permute-start | bytes 3145736 | tf_op jit(solution)/shard_map/ppermute | solution.py:28
  12.4 39.0 %collective-permute-start.2 = (f32[512,512]{1,0:T(8,128)}, f32[512,512]{1,0:T(8,128)S(1)}, u32[]{:S(2)}, u32[]{:S(2)}) collective-permute-start(f32[512,512]{1,0:T(8,128)} %bitcast.23), channel_id=1, source_target_pairs={{0,1},{1,2},{2,3},{3,4},{4,5},{5,6},{6,7},{7,8},{8,9},{9,10},{10,1... | collective-permute-start | bytes 3145736 | tf_op jit(solution)/shard_map/ppermute | solution.py:27
  12.4 0.7 copy-start.11
  13.1 0.7 copy-start.12
  13.7 0.7 copy-start.13
  26.1 2.1 copy-start.1
  28.2 23.2 %copy-start.17 = (f32[512,512]{1,0:T(8,128)}, f32[512,512]{1,0:T(8,128)S(1)}, u32[]{:S(2)}) copy-start(f32[512,512]{1,0:T(8,128)S(1)} %multiply_add_fusion.p1_ref) | copy-start | bytes 3145732
  28.3 31.6 %collective-permute-start.5 = (f32[512,512]{1,0:T(8,128)S(1)}, f32[512,512]{1,0:T(8,128)S(1)}, u32[]{:S(2)}, u32[]{:S(2)}) collective-permute-start(f32[512,512]{1,0:T(8,128)S(1)} %multiply_add_fusion.p1_ref), channel_id=1, source_target_pairs={{1,0},{2,1},{3,2},{4,3},{5,4},{6,5},{7,6},{8,7},{9,8},{10,9},{11,1... | collective-permute-start | bytes 3145736 | tf_op jit(solution)/shard_map/ppermute | solution.py:28
  33.6 26.2 %collective-permute-start.4 = (f32[512,512]{1,0:T(8,128)S(1)}, f32[512,512]{1,0:T(8,128)S(1)}, u32[]{:S(2)}, u32[]{:S(2)}) collective-permute-start(f32[512,512]{1,0:T(8,128)S(1)} %multiply_add_fusion.p1_ref), channel_id=1, source_target_pairs={{0,1},{1,2},{2,3},{3,4},{4,5},{5,6},{6,7},{7,8},{8,9},{9,10},{10,1... | collective-permute-start | bytes 3145736 | tf_op jit(solution)/shard_map/ppermute | solution.py:27
  51.4 1.0 copy-start.20
  51.4 1.3 copy-start.21
  52.7 30.5 %copy-start.7 = (bf16[2,512,512]{2,1,0:T(8,128)(2,1)S(1)}, bf16[2,512,512]{2,1,0:T(8,128)(2,1)}, u32[]{:S(2)}) copy-start(bf16[2,512,512]{2,1,0:T(8,128)(2,1)} %constant.31.clone.y_ref) | copy-start | bytes 3145732
  52.7 30.5 %copy-start.10 = (bf16[512,256]{1,0:T(8,128)(2,1)S(1)}, bf16[512,256]{1,0:T(8,128)(2,1)}, u32[]{:S(2)}) copy-start(bf16[512,256]{1,0:T(8,128)(2,1)} %constant.27.clone.x_ref) | copy-start | bytes 786436
  57.8 1.1 copy-start.6
  58.9 1.0 copy-start.8
  59.8 23.4 %copy-start.22 = (f32[512,512]{1,0:T(8,128)}, f32[512,512]{1,0:T(8,128)S(1)}, u32[]{:S(2)}) copy-start(f32[512,512]{1,0:T(8,128)S(1)} %collective-permute-done.5.rest_3_) | copy-start | bytes 3145732
  59.8 23.3 %copy-start.23 = (f32[512,512]{1,0:T(8,128)}, f32[512,512]{1,0:T(8,128)S(1)}, u32[]{:S(2)}) copy-start(f32[512,512]{1,0:T(8,128)S(1)} %collective-permute-done.4.rest_2_) | copy-start | bytes 3145732
  59.8 38.3 %collective-permute-start.7 = (f32[512,512]{1,0:T(8,128)S(1)}, f32[512,512]{1,0:T(8,128)S(1)}, u32[]{:S(2)}, u32[]{:S(2)}) collective-permute-start(f32[512,512]{1,0:T(8,128)S(1)} %get-tuple-element.35), channel_id=1, source_target_pairs={{1,0},{2,1},{3,2},{4,3},{5,4},{6,5},{7,6},{8,7},{9,8},{10,9},{11,1... | collective-permute-start | bytes 3145736 | tf_op jit(solution)/shard_map/ppermute | solution.py:28
  59.9 38.3 %collective-permute-start.6 = (f32[512,512]{1,0:T(8,128)S(1)}, f32[512,512]{1,0:T(8,128)S(1)}, u32[]{:S(2)}, u32[]{:S(2)}) collective-permute-start(f32[512,512]{1,0:T(8,128)S(1)} %get-tuple-element.35), channel_id=1, source_target_pairs={{0,1},{1,2},{2,3},{3,4},{4,5},{5,6},{6,7},{7,8},{8,9},{9,10},{10,1... | collective-permute-start | bytes 3145736 | tf_op jit(solution)/shard_map/ppermute | solution.py:27
  98.2 1.0 copy-start.18
  99.1 1.0 copy-start.19
  100.1 15.1 %copy-start.15 = (bf16[512,256]{1,0:T(8,128)(2,1)S(1)}, bf16[512,256]{1,0:T(8,128)(2,1)}, u32[]{:S(2)}) copy-start(bf16[512,256]{1,0:T(8,128)(2,1)} %constant.28.clone.x_ref) | copy-start | bytes 786436
  100.1 75.2 %all-to-all-start = ((f32[32,20,8,128]{3,2,1,0:T(8,128)}), f32[32,20,8,128]{3,2,1,0:T(8,128)}, u32[]{:S(2)}, u32[]{:S(2)}) async-start(f32[32,20,8,128]{3,2,1,0:T(8,128)} %get-tuple-element.38), calls=%async_computation | async-start | bytes 5242880 | tf_op jit(solution)/shard_map/all_to_all | solution.py:448
  175.3 64.2 %all-to-all-start.1 = ((f32[32,20,8,128]{3,2,1,0:T(8,128)}), f32[32,20,8,128]{3,2,1,0:T(8,128)S(1)}, u32[]{:S(2)}, u32[]{:S(2)}) async-start(f32[32,20,8,128]{3,2,1,0:T(8,128)} %shard_map.161), calls=%async_computation.1 | async-start | bytes 5242880 | tf_op jit(solution)/shard_map/all_to_all | solution.py:448
  239.5 1.5 copy-start.16
  241.0 64.2 %all-to-all-start.3 = ((f32[32,20,8,128]{3,2,1,0:T(8,128)}), f32[32,20,8,128]{3,2,1,0:T(8,128)S(1)}, u32[]{:S(2)}, u32[]{:S(2)}) async-start(f32[32,20,8,128]{3,2,1,0:T(8,128)} %shard_map.160), calls=%async_computation.3 | async-start | bytes 5242880 | tf_op jit(solution)/shard_map/all_to_all | solution.py:448
  249.5 1.5 copy-start
  305.1 1.5 copy-start.2
  306.6 64.3 %all-to-all-start.2 = ((f32[32,20,8,128]{3,2,1,0:T(8,128)}), f32[32,20,8,128]{3,2,1,0:T(8,128)S(1)}, u32[]{:S(2)}, u32[]{:S(2)}) async-start(f32[32,20,8,128]{3,2,1,0:T(8,128)} %copy-done), calls=%async_computation.2 | async-start | bytes 5242880 | tf_op jit(solution)/shard_map/all_to_all | solution.py:448
  310.8 3.8 %copy-start.3 = (f32[32,20,8,128]{3,2,1,0:T(8,128)S(1)}, f32[32,20,8,128]{3,2,1,0:T(8,128)}, u32[]{:S(2)}) copy-start(f32[32,20,8,128]{3,2,1,0:T(8,128)} %copy-done.2) | copy-start | bytes 7864324
  310.8 3.8 copy-start.4
  310.8 3.8 copy-start.14
  314.6 56.2 %copy-start.9 = (bf16[512,256]{1,0:T(8,128)(2,1)S(1)}, bf16[512,256]{1,0:T(8,128)(2,1)}, u32[]{:S(2)}) copy-start(bf16[512,256]{1,0:T(8,128)(2,1)} %constant.30.clone.x_ref) | copy-start | bytes 786436
  370.9 1.2 copy-start.5
